TPU v7x, 512 devices: a whole 4x4x16 slice. The times are simulated.
512 devices in a mesh: dp: 64 (over z, y_lo, core), mp: 8 (over x, y_hi).
Axes of the slice: x: 4, y: 4 (y_hi: 2, y_lo: 2; y = y_hi * 2 + y_lo), z: 16, core: 2. Of those that a mesh axis runs over, the one named last changes fastest.
Arguments:
- attn_out: bfloat16 [16384, 7168], P('dp', 'mp'), may hold values from -6 to 6
- out_grad: bfloat16 [16384, 7168], P('dp', 'mp'), may hold values from -6 to 6
- projection: bfloat16 [7168, 256], P('dp'), may hold values from -0.0625 to 0.0625
- momentum: float32 [7168, 256], P('mp'), may hold values from -6 to 6
- weight: bfloat16 [7168, 7168], P('mp', 'dp'), may hold values from -6 to 6
Outputs:
- new_momentum: float32 [7168, 256], P('mp')
- new_weight: bfloat16 [7168, 7168], P('mp', 'dp')
All inputs are finite; a program needn't handle non-finite values.
Results may differ from a plain program's by a relative error of at most 0.0075.
Values may be sent and summed in bfloat16 or wider, within the bound.
A program may use at most 128 MiB of HBM per device.

v0:
```python
import math

import jax
import jax.numpy as jnp
from jax import lax
from jax.sharding import PartitionSpec as P


def shards(attn_out, out_grad, projection, momentum, weight):
    tok_rows = attn_out.shape[0]
    factor = 1.0 / math.sqrt(tok_rows * lax.axis_size("dp"))
    whole_grad = lax.all_gather(out_grad, "mp", axis=1, tiled=True)
    grad_block = lax.dot_general(
        attn_out, whole_grad, (((0,), (0,)), ((), ())), preferred_element_type=jnp.float32
    )
    compressed_local = jnp.dot(
        grad_block,
        lax.all_gather(projection, "dp", axis=0, tiled=True).astype(jnp.float32),
        precision=lax.Precision.HIGHEST,
    )
    compressed = lax.psum(compressed_local * factor, "dp")
    new_momentum = 0.9 * momentum + compressed
    update = jnp.dot(
        new_momentum, projection.astype(jnp.float32).T, precision=lax.Precision.HIGHEST
    )
    new_weight = (weight.astype(jnp.float32) - 2.0 * update).astype(jnp.bfloat16)
    return (new_momentum, new_weight)


def solution(mesh):
    return jax.shard_map(
        shards,
        mesh=mesh,
        in_specs=(P("dp", "mp"), P("dp", "mp"), P("dp", None), P("mp", None), P("mp", "dp")),
        out_specs=(P("mp", None), P("mp", "dp")),
        check_vma=False,
    )
```

profile of v0, /device:TPU:1, one launch (start us, length us, event | category | flops | bytes accessed | tf_op | source)
XLA Modules:
  0.0 675.0 jit_solution(7446995630826475373)
XLA Ops:
  7.2 0.0 copy-start
  7.2 0.0 all-gather.3.cloned.1.call-start
  7.2 0.7 all-gather.3.cloned.1.call-update
  7.9 0.0 all-gather.5.cloned.1.call-start
  8.0 0.7 all-gather.5.cloned.1.call-update
  8.7 0.0 all-reduce.2.cloned.1.call-start
  8.7 89.7 %all-gather.3.cloned.1.call-done = bf16[256,7168]{1,0:T(8,128)(2,1)} async-done(((bf16[256,896]{1,0:T(8,128)(2,1)}), bf16[256,7168]{1,0:T(8,128)(2,1)}) %all-gather.3.cloned.1.call-update) | async-done | bytes 3670032 | tf_op jit(solution)/shard_map/all_gather | solution.py:12
  98.4 0.0 copy-done
  98.4 14.0 %fusion.2 = f32[896,7168]{1,0:T(8,128)} fusion(bf16[256,896]{1,0:T(8,128)(2,1)S(1)} %copy-done, bf16[256,7168]{1,0:T(8,128)(2,1)} %all-gather.3.cloned.1.call-done), kind=kOutput, calls=%fused_computation.5 | convolution fusion | flops 3288334336 | bytes 29818880 | tf_op jit(solution)/shard_map/dot_general | solution.py:13
  112.5 0.0 copy-start.2
  112.5 110.8 %all-gather.5.cloned.1.call-done = bf16[7168,256]{1,0:T(8,128)(2,1)} async-done(((bf16[112,256]{1,0:T(8,128)(2,1)}), bf16[7168,256]{1,0:T(8,128)(2,1)}) %all-gather.5.cloned.1.call-update) | async-done | bytes 3670032 | tf_op jit(solution)/shard_map/all_gather | solution.py:18
  223.3 16.7 %convolution_multiply_fusion = f32[896,256]{1,0:T(8,128)} fusion(f32[896,7168]{1,0:T(8,128)} %fusion.2, bf16[7168,256]{1,0:T(8,128)(2,1)} %all-gather.5.cloned.1.call-done), kind=kOutput, calls=%fused_computation | convolution fusion | flops 19730235392 | bytes 30277632 | tf_op jit(solution)/shard_map/dot_general | solution.py:16
  240.0 0.0 copy-start.3
  240.0 0.0 copy-start.4
  240.0 0.0 all-reduce.2.cloned.1.call-update
  240.0 425.8 %all-reduce.2.cloned.1.call-done = f32[896,256]{1,0:T(8,128)} async-done(((f32[896,256]{1,0:T(8,128)}), f32[896,256]{1,0:T(8,128)}) %all-reduce.2.cloned.1.call-update) | async-done | bytes 917520 | tf_op jit(solution)/shard_map/psum | solution.py:21
  665.8 0.0 copy-done.2
  665.8 1.3 multiply_add_fusion
  667.1 0.0 copy-done.3
  667.1 0.0 copy-done.4
  667.1 0.0 copy-start.1
  667.1 1.3 fusion.1
  668.4 0.0 copy-done.1
Async XLA Ops:
  7.2 91.3 %copy-start = (bf16[256,896]{1,0:T(8,128)(2,1)S(1)}, bf16[256,896]{1,0:T(8,128)(2,1)}, u32[]{:S(2)}) copy-start(bf16[256,896]{1,0:T(8,128)(2,1)} %param.5) | copy-start | bytes 1376260
  7.2 91.2 %all-gather.3.cloned.1.call-start = ((), (), s32[]{:S(2)}) async-start(), calls=%async_computation | async-start | bytes 4128768 | tf_op jit(solution)/shard_map/all_gather | solution.py:12
  7.9 215.4 %all-gather.5.cloned.1.call-start = ((), (), s32[]{:S(2)}) async-start(), calls=%async_computation.1 | async-start | bytes 3727360 | tf_op jit(solution)/shard_map/all_gather | solution.py:18
  8.7 657.1 %all-reduce.2.cloned.1.call-start = ((), (), s32[]{:S(2)}) async-start(), calls=%async_computation.2 | async-start | bytes 1835008 | tf_op jit(solution)/shard_map/psum | solution.py:21
  112.5 553.3 %copy-start.2 = (f32[896,256]{1,0:T(8,128)S(1)}, f32[896,256]{1,0:T(8,128)}, u32[]{:S(2)}) copy-start(f32[896,256]{1,0:T(8,128)} %param.8) | copy-start | bytes 2752516
  240.0 427.1 %copy-start.3 = (bf16[112,256]{1,0:T(8,128)(2,1)S(1)}, bf16[112,256]{1,0:T(8,128)(2,1)}, u32[]{:S(2)}) copy-start(bf16[112,256]{1,0:T(8,128)(2,1)} %param.7) | copy-start | bytes 172036
  240.0 427.1 %copy-start.4 = (bf16[896,112]{0,1:T(8,128)(2,1)S(1)}, bf16[896,112]{0,1:T(8,128)(2,1)}, u32[]{:S(2)}) copy-start(bf16[896,112]{0,1:T(8,128)(2,1)} %param.9) | copy-start | bytes 602116
  667.1 1.3 copy-start.1
Sparse Core Ops, SparseCore 0:
  11.2 87.1 all-gather.2
  100.6 122.6 all-gather.4
  240.1 425.6 all-reduce.1
where the time goes:
time: 675 us
  waiting for transfers between devices  628 us (93%)
  matrix products  32 us (5%)
  between operations  13.8 us (2%)
    psum x1, waiting for transfers between devices, shards(): compressed = lax.psum(compressed_local * factor, 'dp')  426 us
    all_gather x1, waiting for transfers between devices, shards(): lax.all_gather(projection, 'dp', axis=0, tiled=True).astype(jnp.float32)  111 us
    all_gather x1, waiting for transfers between devices, shards(): whole_grad = lax.all_gather(out_grad, 'mp', axis=1, tiled=True)  89.7 us
    dot_general x1, matrix products, shards(): jnp.dot(grad_block, lax.all_gather(projection, 'dp', axis=0, tiled=True)....  16.7 us
    dot_general x1, matrix products, shards(): lax.dot_general(attn_out, whole_grad, (((0,), (0,)), ((), ())), preferred...  14 us
  transfers between devices with their start and end apart: 3, of which 3 were waited for; matrix products, arithmetic and copies ran while one was open for 2% of the time, Pallas kernels for 0%

commit v1 on v0

v1 whole, which is shorter than its diff:
```python
import math

import jax
import jax.numpy as jnp
from jax import lax
from jax.sharding import PartitionSpec as P


def shards(attn_out, out_grad, projection, momentum, weight):
    tok_rows = attn_out.shape[0]
    cols = out_grad.shape[1]
    factor = 1.0 / math.sqrt(tok_rows * lax.axis_size("dp"))
    whole = lax.all_gather(projection, "dp", axis=0, tiled=True)
    mine = lax.dynamic_slice_in_dim(whole, lax.axis_index("mp") * cols, cols, axis=0)
    part = jnp.dot(out_grad, mine, preferred_element_type=jnp.float32)
    reduced = lax.psum(part, "mp").astype(jnp.bfloat16)
    compressed_local = lax.dot_general(
        attn_out, reduced, (((0,), (0,)), ((), ())), preferred_element_type=jnp.float32
    )
    compressed = lax.psum(compressed_local * factor, "dp")
    new_momentum = 0.9 * momentum + compressed
    update = lax.dot_general(
        new_momentum.astype(jnp.bfloat16),
        projection,
        (((1,), (1,)), ((), ())),
        preferred_element_type=jnp.float32,
    )
    new_weight = (weight.astype(jnp.float32) - 2.0 * update).astype(jnp.bfloat16)
    return (new_momentum, new_weight)


def solution(mesh):
    return jax.shard_map(
        shards,
        mesh=mesh,
        in_specs=(P("dp", "mp"), P("dp", "mp"), P("dp", None), P("mp", None), P("mp", "dp")),
        out_specs=(P("mp", None), P("mp", "dp")),
        check_vma=False,
    )
```

time: 675 us -> 619 us (0.917)
  waiting for transfers between devices: 628 us -> 561 us
  blocking collectives: 0 us -> 37.4 us
  matrix products: 32 us -> 3.63 us
    all_gather x2 -> x1, waiting for transfers between devices: 201 us -> 132 us  [shards(): whole = lax.all_gather(projection, 'dp', axis=0, tiled=True)]
    psum x0 -> x1, blocking collectives: none -> 37.4 us  [shards(): reduced = lax.psum(part, 'mp').astype(jnp.bfloat16)]
    dot_general x3, matrix products: 32 us -> 3.63 us  [the longest x1 1.5 us: shards(): part = jnp.dot(out_grad, mine, preferred_element_type=jnp.float32)]
  transfers between devices with their start and end apart: 3 -> 2, of which waited for: 3 -> 2; matrix products, arithmetic and copies ran while one was open for 2% -> 0% of each run, Pallas kernels for 0% -> 0%
where the time goes in v1:
time: 619 us
  waiting for transfers between devices  561 us (91%)
  blocking collectives  37.4 us (6%)
  between operations  14.1 us (2%)
    psum x1, waiting for transfers between devices, shards(): compressed = lax.psum(compressed_local * factor, 'dp')  428 us
    all_gather x1, waiting for transfers between devices, shards(): whole = lax.all_gather(projection, 'dp', axis=0, tiled=True)  132 us
    psum x1, blocking collectives, shards(): reduced = lax.psum(part, 'mp').astype(jnp.bfloat16)  37.4 us
  transfers between devices with their start and end apart: 2, of which 2 were waited for; matrix products, arithmetic and copies ran while one was open for 0% of the time, Pallas kernels for 0%

profile of v1, /device:TPU:1, one launch (start us, length us, event | category | flops | bytes accessed | tf_op | source)
XLA Modules:
  0.0 618.8 jit_solution(12834203399609337722)
XLA Ops:
  7.2 0.0 copy-start
  7.2 0.0 copy-start.1
  7.2 0.0 all-gather.2.cloned.1.call-start
  7.2 0.7 all-gather.2.cloned.1.call-update
  7.9 0.0 all-reduce.3.cloned.1.call-start
  8.0 131.8 %all-gather.2.cloned.1.call-done = bf16[7168,256]{1,0:T(8,128)(2,1)} async-done(((bf16[112,256]{1,0:T(8,128)(2,1)}), bf16[7168,256]{1,0:T(8,128)(2,1)}) %all-gather.2.cloned.1.call-update) | async-done | bytes 3670032 | tf_op jit(solution)/shard_map/all_gather | solution.py:13
  139.8 1.5 convolution_bitcast_fusion
  141.3 37.4 %all-reduce.4 = bf16[256,256]{0,1:T(8,128)(2,1)S(1)} all-reduce(f32[256,256]{0,1:T(8,128)S(1)} %convolution_bitcast_fusion), channel_id=1, replica_groups=mesh['dp'=64,'mp'=8] {'mp'}, use_global_device_ids=true, to_apply=%region_0.0 | all-reduce | flops 65536 | bytes 393216 | tf_op jit(solution)/shard_map/psum | solution.py:16
  178.7 0.0 copy-done
  178.7 1.2 fusion
  179.9 0.0 copy-start.2
  179.9 0.0 copy-start.3
  179.9 0.0 all-reduce.3.cloned.1.call-update
  180.0 0.0 copy-done.1
  180.0 0.3 copy.7
  180.3 428.2 %all-reduce.3.cloned.1.call-done = f32[896,256]{0,1:T(8,128)} async-done(((f32[896,256]{0,1:T(8,128)}), f32[896,256]{0,1:T(8,128)}) %all-reduce.3.cloned.1.call-update) | async-done | bytes 917520 | tf_op jit(solution)/shard_map/psum | solution.py:20
  608.5 1.3 multiply_add_fusion
  609.8 1.2 copy.8
  611.0 0.0 copy-done.2
  611.0 0.0 copy-done.3
  611.0 0.9 fusion.2
Async XLA Ops:
  7.2 171.5 %copy-start = (bf16[256,896]{1,0:T(8,128)(2,1)S(1)}, bf16[256,896]{1,0:T(8,128)(2,1)}, u32[]{:S(2)}) copy-start(bf16[256,896]{1,0:T(8,128)(2,1)} %param.5) | copy-start | bytes 1376260
  7.2 172.8 %copy-start.1 = (f32[896,256]{1,0:T(8,128)S(1)}, f32[896,256]{1,0:T(8,128)}, u32[]{:S(2)}) copy-start(f32[896,256]{1,0:T(8,128)} %param.8) | copy-start | bytes 2752516
  7.2 132.6 %all-gather.2.cloned.1.call-start = ((), (), s32[]{:S(2)}) async-start(), calls=%async_computation | async-start | bytes 3727360 | tf_op jit(solution)/shard_map/all_gather | solution.py:13
  7.9 600.6 %all-reduce.3.cloned.1.call-start = ((), (), s32[]{:S(2)}) async-start(), calls=%async_computation.1 | async-start | bytes 1835008 | tf_op jit(solution)/shard_map/psum | solution.py:20
  179.9 431.1 %copy-start.2 = (bf16[112,256]{1,0:T(8,128)(2,1)S(1)}, bf16[112,256]{1,0:T(8,128)(2,1)}, u32[]{:S(2)}) copy-start(bf16[112,256]{1,0:T(8,128)(2,1)} %param.7) | copy-start | bytes 172036
  179.9 431.1 %copy-start.3 = (bf16[896,112]{0,1:T(8,128)(2,1)S(1)}, bf16[896,112]{0,1:T(8,128)(2,1)}, u32[]{:S(2)}) copy-start(bf16[896,112]{0,1:T(8,128)(2,1)} %param.9) | copy-start | bytes 602116
Sparse Core Ops, SparseCore 0:
  10.2 129.5 all-gather.1
  180.1 428.3 all-reduce.2

commit v2 on v0

v2 whole, which is shorter than its diff:
```python
import functools
import math

import jax
import jax.numpy as jnp
from jax import lax
from jax.experimental import pallas as pl
from jax.experimental.pallas import tpu as pltpu
from jax.sharding import PartitionSpec as P

MESH = pl.DeviceIdType.MESH
BF16 = jnp.bfloat16
F32 = jnp.float32

NZ, NM = 16, 8
BLK = 112
SL = 16
SLICES = 7
TOK, COLS, RANK = 256, 896, 256
HALF = RANK // 2
PIECE = TOK // NM
CHUNK = COLS // 8
NEAR = (0, 1, -1, -2)
FAR_FIRST = (8, 7, 9, 6, 10, 5, 11, 4, 12, 3, 13, 2, 14, 1, 15)
NEAR_FIRST = (0, 1, 7, 2, 6, 3, 5, 4)


def kernel(
    factor,
    a_hbm, g_hbm, p_hbm, m_hbm, w_hbm,
    c_out, w_out,
    a, at, g, p, mom, w,
    pz, p2, pfull, part, rs, red,
    cown, csend, crecv, sb, rs2, far, cres,
    in_sem,
    p1s, p1r, p2s, p2r, p3s, p3r,
    r1s, r1r, r2s, r2r,
    d1s, d1r, d2s, d2r, d3s, d3r, d4s, d4r, d5s, d5r,
):
    dp, m = lax.axis_index("dp"), lax.axis_index("mp")
    z, yl, core = dp // 4, (dp // 2) % 2, dp % 2
    sign = 1 - 2 * core

    def dev(z_, yl_, core_, m_):
        return ((z_ * 2 + yl_) * 2 + core_, m_)

    sibling = dev(z, yl, 1 - core, m)

    def remote(src, dst, ssem, rsem, to):
        return pltpu.make_async_remote_copy(
            src_ref=src, dst_ref=dst, send_sem=ssem, recv_sem=rsem, device_id=to, device_id_type=MESH
        )

    def arrived(dst, rsem):
        remote(dst, dst, rsem, rsem, sibling).wait_recv()

    sent = []

    def send(src, dst, ssem, rsem, to):
        copy = remote(src, dst, ssem, rsem, to)
        copy.start()
        return copy

    loads = [
        pltpu.make_async_copy(src, dst, in_sem.at[i])
        for i, (src, dst) in enumerate(
            ((p_hbm, p), (a_hbm, a), (g_hbm, g), (m_hbm, mom), (w_hbm, w))
        )
    ]
    for load in loads:
        load.start()

    barrier = pltpu.get_barrier_semaphore()

    def greet(to):
        pl.semaphore_signal(barrier, inc=1, device_id=to, device_id_type=MESH)

    for k in FAR_FIRST:
        greet(dev((z + k) % NZ, yl, core, m))
    for k in range(1, NM):
        greet(dev(z, yl, core, (m + k) % NM))
    for k in range(NM):
        greet(dev(z, 1 - yl, core, (m + k) % NM))
    for k in (2, 14, 1, 15):
        greet(dev((z + k) % NZ, 1 - yl, core, m))
    greet(sibling)

    loads[0].wait()
    loads[1].wait()
    for k in range(COLS // 128):
        at[128 * k : 128 * (k + 1)] = a[:, 128 * k : 128 * (k + 1)].T

    pl.semaphore_wait(barrier, 15 + 7 + 8 + 4 + 1)

    @pl.when(m < SLICES)
    def _():
        rows = pl.ds(pl.multiple_of(jnp.minimum(m, SLICES - 1) * SL, SL), SL)
        pz[z] = p[rows]
        copies = [
            send(p.at[rows], pz.at[z], p1s.at[k], p1r.at[z], dev((z + k) % NZ, yl, core, m))
            for k in FAR_FIRST
        ]
        slot = jnp.minimum(m, SLICES - 1)
        for q in NEAR_FIRST:
            mt = (z // 2 + q) % NM
            for s in range(2):
                zs = 2 * mt + s
                if q == 0:
                    @pl.when(zs != z)
                    def _():
                        arrived(pz.at[zs], p1r.at[zs])
                else:
                    arrived(pz.at[zs], p1r.at[zs])
            src = pz.at[pl.ds(2 * mt, 2)]
            copies.append(
                send(src, p2.at[core, yl, slot], p2s.at[q], p2r.at[yl, slot], dev(z, 1 - yl, core, mt))
            )

            @pl.when(mt != m)
            def _():
                send(src, p2.at[core, yl, slot], p2s.at[NM + q], p2r.at[yl, slot], dev(z, yl, core, mt))

            @pl.when(mt == m)
            def _():
                p2[core, yl, slot] = pz[pl.ds(2 * mt, 2)]

        for copy in copies:
            copy.wait_send()
        for q in NEAR_FIRST:
            mt = (z // 2 + q) % NM

            @pl.when(mt != m)
            def _():
                remote(pz.at[pl.ds(2 * mt, 2)], p2.at[core, yl, slot], p2s.at[NM + q], p2r.at[yl, slot], sibling).wait_send()

    for ms in range(SLICES):
        for ys in range(2):
            @pl.when((ms != m) | (ys != yl))
            def _():
                arrived(p2.at[core, ys, ms], p2r.at[ys, ms])

            sent.append(send(p2.at[core, ys, ms], p2.at[core, ys, ms], p3s.at[ys, ms], p3r.at[ys, ms], sibling))
    for ms in range(SLICES):
        for ys in range(2):
            arrived(p2.at[1 - core, ys, ms], p3r.at[ys, ms])
    for c in range(2):
        for ys in range(2):
            for ms in range(SLICES):
                for s in range(2):
                    at_row = BLK * (4 * s + 2 * ys + c) + SL * ms
                    pfull[at_row : at_row + SL] = p2[c, ys, ms, s]

    loads[2].wait()
    part[...] = jnp.dot(g[...], pfull[...], preferred_element_type=F32).astype(BF16)

    def piece(i):
        return pl.ds(pl.multiple_of(i * PIECE, PIECE), PIECE)

    for k in range(1, NM):
        mt = (m + k) % NM
        sent.append(send(part.at[piece(mt)], rs.at[m], r1s.at[k], r1r.at[m], dev(z, yl, core, mt)))
    rs[m] = part[piece(m)]
    for k in range(1, NM):
        arrived(rs.at[(m + k) % NM], r1r.at[(m + k) % NM])
    total = rs[0].astype(F32)
    for i in range(1, NM):
        total += rs[i].astype(F32)
    red[piece(m)] = total.astype(BF16)
    for k in range(1, NM):
        mt = (m + k) % NM
        sent.append(send(red.at[piece(m)], red.at[piece(m)], r2s.at[k], r2r.at[m], dev(z, yl, core, mt)))
    for k in range(1, NM):
        mt = (m + k) % NM
        arrived(red.at[piece(mt)], r2r.at[mt])

    for k in range(COLS // 128):
        rows = slice(128 * k, 128 * (k + 1))
        tile = jnp.dot(at[rows], red[...], preferred_element_type=F32)
        low, high = tile[:, :HALF], tile[:, HALF:]
        cown[rows] = jnp.where(core == 0, low, high)
        csend[rows] = jnp.where(core == 0, high, low).astype(BF16)
    sent.append(send(csend, crecv, d1s, d1r, sibling))
    arrived(crecv, d1r)
    sb[...] = (cown[...] + crecv[...].astype(F32)).astype(BF16)

    def chunk(z_, yl_):
        return pl.ds(pl.multiple_of((2 * (z_ % 4) + yl_) * CHUNK, SL), CHUNK)

    for i in (3, 1, 2, 0):
        zo = (z + sign * NEAR[i] + NZ) % NZ
        for other in (1, 0):
            if i == 0 and other == 0:
                continue
            yo = (yl + other) % 2
            sent.append(
                send(sb.at[chunk(zo, yo)], rs2.at[i, yl], d2s.at[i, other], d2r.at[i, yl], dev(zo, yo, core, m))
            )
    rs2[0, yl] = sb[chunk(z, yl)]
    arrived(rs2.at[0, 1 - yl], d2r.at[0, 1 - yl])
    for i in (1, 2, 3):
        for y in range(2):
            arrived(rs2.at[i, y], d2r.at[i, y])
    total = rs2[0, 0].astype(F32) + rs2[0, 1].astype(F32)
    for i in (1, 2, 3):
        total += rs2[i, 0].astype(F32) + rs2[i, 1].astype(F32)
    zh = z // 4
    far[zh] = total.astype(BF16)
    for k in (2, 1, 3):
        sent.append(send(far.at[zh], far.at[zh], d3s.at[k], d3r.at[zh], dev((z + 4 * k) % NZ, yl, core, m)))
    for k in (1, 3, 2):
        arrived(far.at[(zh + k) % 4], d3r.at[(zh + k) % 4])
    total = far[0].astype(F32)
    for i in range(1, 4):
        total += far[i].astype(F32)
    own = chunk(z, yl)
    cres[core, own] = (total * factor).astype(BF16)
    for i in (3, 1, 2, 0):
        zu = (z - sign * NEAR[i] + NZ) % NZ
        for other in (1, 0):
            if i == 0 and other == 0:
                continue
            yu = (yl + other) % 2
            sent.append(
                send(cres.at[core, own], cres.at[core, own], d4s.at[i, other], d4r.at[i, yl], dev(zu, yu, core, m))
            )
    sent.append(send(cres.at[core, own], cres.at[core, own], d5s.at[0, 0], d5r.at[0, 0], sibling))
    for i in (0, 1, 2, 3):
        zo = (z + sign * NEAR[i] + NZ) % NZ
        for other in (0, 1):
            if i == 0 and other == 0:
                continue
            yo = (yl + other) % 2
            place = cres.at[core, chunk(zo, yo)]
            arrived(place, d4r.at[i, yo])
            sent.append(send(place, place, d5s.at[i, other], d5r.at[i, other], sibling))
    for i in (0, 1, 2, 3):
        zo = (z - sign * NEAR[i] + NZ) % NZ
        for other in (0, 1):
            arrived(cres.at[1 - core, chunk(zo, (yl + other) % 2)], d5r.at[i, other])

    loads[3].wait()
    loads[4].wait()
    for k in range(COLS // 128):
        rows = slice(128 * k, 128 * (k + 1))
        both = jnp.concatenate([cres[0, rows], cres[1, rows]], axis=1)
        c_out[rows] = both
        new_mom = (0.9 * mom[rows] + both.astype(F32)).astype(BF16)
        update = lax.dot_general(new_mom, p[...], (((1,), (1,)), ((), ())), preferred_element_type=F32)
        w_out[rows] = (w[rows].astype(F32) - 2.0 * update).astype(BF16)
    for copy in sent:
        copy.wait_send()


def shards(attn_out, out_grad, projection, momentum, weight):
    factor = 1.0 / math.sqrt(attn_out.shape[0] * lax.axis_size("dp"))
    vmem, dma = pltpu.VMEM, pltpu.SemaphoreType.DMA
    compressed, new_weight = pl.pallas_call(
        functools.partial(kernel, factor),
        out_shape=(
            jax.ShapeDtypeStruct((COLS, RANK), BF16),
            jax.ShapeDtypeStruct((COLS, BLK), BF16),
        ),
        in_specs=[pl.BlockSpec(memory_space=pl.ANY)] * 5,
        out_specs=(pl.BlockSpec(memory_space=vmem), pl.BlockSpec(memory_space=vmem)),
        scratch_shapes=[
            vmem((TOK, COLS), BF16), vmem((COLS, TOK), BF16), vmem((TOK, COLS), BF16),
            vmem((BLK, RANK), BF16), vmem((COLS, RANK), F32), vmem((COLS, BLK), BF16),
            vmem((NZ, SL, RANK), BF16), vmem((2, 2, SLICES, 2, SL, RANK), BF16), vmem((COLS, RANK), BF16),
            vmem((TOK, RANK), BF16), vmem((NM, PIECE, RANK), BF16), vmem((TOK, RANK), BF16),
            vmem((COLS, HALF), F32), vmem((COLS, HALF), BF16), vmem((COLS, HALF), BF16),
            vmem((COLS, HALF), BF16), vmem((4, 2, CHUNK, HALF), BF16), vmem((4, CHUNK, HALF), BF16),
            vmem((2, COLS, HALF), BF16),
            dma((5,)),
            dma((NZ,)), dma((NZ,)), dma((2 * NM,)), dma((2, SLICES)), dma((2, SLICES)), dma((2, SLICES)),
            dma((NM,)), dma((NM,)), dma((NM,)), dma((NM,)),
            dma, dma, dma((4, 2)), dma((4, 2)), dma((4,)), dma((4,)),
            dma((4, 2)), dma((4, 2)), dma((4, 2)), dma((4, 2)),
        ],
        compiler_params=pltpu.CompilerParams(
            collective_id=0, has_side_effects=True, vmem_limit_bytes=32 * 2**20
        ),
        cost_estimate=pl.CostEstimate(flops=300_000_000, bytes_accessed=4_000_000, transcendentals=0),
        name="reduce_and_step",
    )(attn_out, out_grad, projection, momentum, weight)
    new_momentum = 0.9 * momentum + compressed.astype(F32)
    return (new_momentum, new_weight)


def solution(mesh):
    return jax.shard_map(
        shards,
        mesh=mesh,
        in_specs=(P("dp", "mp"), P("dp", "mp"), P("dp", None), P("mp", None), P("mp", "dp")),
        out_specs=(P("mp", None), P("mp", "dp")),
        check_vma=False,
    )
```

time: 675 us -> 75.1 us (0.11)
  waiting for transfers between devices: 628 us -> 0 us
  Pallas kernels: 0 us -> 68 us
  matrix products: 32 us -> 0 us
  between operations: 13.8 us -> 0.67 us
    psum x1 -> x0, waiting for transfers between devices: 426 us -> none  [shards(): compressed = lax.psum(compressed_local * factor, 'dp')]
    all_gather x2 -> x0, waiting for transfers between devices: 201 us -> none  [the longest x1 111 us: shards(): lax.all_gather(projection, 'dp', axis=0, tiled=True).astype(jnp.float32)]
    pallas_call x0 -> x1, Pallas kernels: none -> 68 us  [shards(): pl.pallas_call(functools.partial(kernel, factor), out_shape=(jax.ShapeDty...]
    dot_general x3 -> x0, matrix products: 32 us -> none  [the longest x1 16.7 us: shards(): jnp.dot(grad_block, lax.all_gather(projection, 'dp', axis=0, tiled=True)....]
  transfers between devices with their start and end apart: 3 -> 0, of which waited for: 3 -> 0; matrix products, arithmetic and copies ran while one was open for 2% -> 0% of each run, Pallas kernels for 0% -> 0%
where the time goes in v2:
time: 75.1 us; the launch traced here: 74.8 us
  Pallas kernels  68 us (91%)
  local copies, waits for them, and re-layouts  5.15 us (7%)
  other arithmetic  1.02 us (1%)
    pallas_call x1, Pallas kernels, shards(): pl.pallas_call(functools.partial(kernel, factor), out_shape=(jax.ShapeDty...  68 us
    unnamed x12, local copies, waits for them, and re-layouts  5.15 us

profile of v2, /device:TPU:1, one launch (start us, length us, event | category | flops | bytes accessed | tf_op | source)
XLA Modules:
  0.0 74.8 jit_solution(14101306485509924167)
XLA Ops:
  0.6 0.0 copy-start.4
  0.6 1.1 %copy.7.w_hbm = bf16[896,112]{1,0:T(8,128)(2,1)S(1)} copy(bf16[896,112]{0,1:T(8,128)(2,1)} %param.9) | data formatting | bytes 401408 | tf_op args[4]
  1.8 0.0 copy-done.4
  1.8 0.0 copy-start
  1.8 1.2 %copy-done = f32[896,256]{1,0:T(8,128)S(1)} copy-done((f32[896,256]{1,0:T(8,128)S(1)}, f32[896,256]{1,0:T(8,128)}, u32[]{:S(2)}) %copy-start) | copy-done | bytes 917528
  2.9 0.0 copy-start.2
  2.9 1.0 %copy-done.2 = bf16[256,896]{1,0:T(8,128)(2,1)S(1)} copy-done((bf16[256,896]{1,0:T(8,128)(2,1)S(1)}, bf16[256,896]{1,0:T(8,128)(2,1)}, u32[]{:S(2)}) %copy-start.2) | copy-done | bytes 458776
  4.0 0.0 copy-start.3
  4.0 1.0 %copy-done.3 = bf16[256,896]{1,0:T(8,128)(2,1)S(1)} copy-done((bf16[256,896]{1,0:T(8,128)(2,1)S(1)}, bf16[256,896]{1,0:T(8,128)(2,1)}, u32[]{:S(2)}) %copy-start.3) | copy-done | bytes 458776
  5.0 0.0 copy-start.1
  5.0 68.0 %reduce_and_step.1 = (bf16[896,256]{1,0:T(8,128)(2,1)S(1)}, bf16[896,112]{1,0:T(8,128)(2,1)S(1)}) custom-call(bf16[256,896]{1,0:T(8,128)(2,1)S(1)} %copy-done.2, bf16[256,896]{1,0:T(8,128)(2,1)S(1)} %copy-done.3, bf16[112,256]{1,0:T(8,128)(2,1)S(1)} %copy-done.4, f32[896,256]{1,0:T(8,128)S(1)} %copy-done, bf16[896,112]{1,0:T(8,128)(2,1)S(1)} %copy.7.w_hbm), custom_call_target="tpu_custom_call" | custom-call | flops 300000000 | bytes 4000000 | tf_op jit(solution)/shard_map/reduce_and_step/pallas_call | solution.py:257
  73.0 0.8 %copy.8 = bf16[896,112]{0,1:T(8,128)(2,1)} copy(bf16[896,112]{1,0:T(8,128)(2,1)S(1)} %get-tuple-element.7) | data formatting | bytes 401408
  73.8 0.0 copy-done.1
  73.8 1.0 %convert_add_fusion = f32[896,256]{1,0:T(8,128)} fusion(bf16[896,256]{1,0:T(8,128)(2,1)S(1)} %get-tuple-element.4, f32[896,256]{1,0:T(8,128)S(1)} %copy-done.1), kind=kLoop, calls=%fused_computation | loop fusion | flops 688128 | bytes 2293760 | tf_op jit(solution)/shard_map/add | solution.py:285
Async XLA Ops:
  0.6 1.1 %copy-start.4 = (bf16[112,256]{1,0:T(8,128)(2,1)S(1)}, bf16[112,256]{1,0:T(8,128)(2,1)}, u32[]{:S(2)}) copy-start(bf16[112,256]{1,0:T(8,128)(2,1)} %p_hbm.1) | copy-start | bytes 172036
  1.8 1.2 %copy-start = (f32[896,256]{1,0:T(8,128)S(1)}, f32[896,256]{1,0:T(8,128)}, u32[]{:S(2)}) copy-start(f32[896,256]{1,0:T(8,128)} %m_hbm.1) | copy-start | bytes 2752516
  2.9 1.0 %copy-start.2 = (bf16[256,896]{1,0:T(8,128)(2,1)S(1)}, bf16[256,896]{1,0:T(8,128)(2,1)}, u32[]{:S(2)}) copy-start(bf16[256,896]{1,0:T(8,128)(2,1)} %a_hbm.1) | copy-start | bytes 1376260
  4.0 1.0 %copy-start.3 = (bf16[256,896]{1,0:T(8,128)(2,1)S(1)}, bf16[256,896]{1,0:T(8,128)(2,1)}, u32[]{:S(2)}) copy-start(bf16[256,896]{1,0:T(8,128)(2,1)} %g_hbm.1) | copy-start | bytes 1376260
  5.0 68.8 %copy-start.1 = (f32[896,256]{1,0:T(8,128)S(1)}, f32[896,256]{1,0:T(8,128)}, u32[]{:S(2)}) copy-start(f32[896,256]{1,0:T(8,128)} %m_hbm.1) | copy-start | bytes 2752516

commit v3 on v2

v3 whole, which is shorter than its diff:
```python
import functools
import math

import jax
import jax.numpy as jnp
from jax import lax
from jax.experimental import pallas as pl
from jax.experimental.pallas import tpu as pltpu
from jax.sharding import PartitionSpec as P

MESH = pl.DeviceIdType.MESH
BF16 = jnp.bfloat16
F32 = jnp.float32

NZ, NM = 16, 8
BLK = 112
SL = 16
SLICES = 7
TOK, COLS, RANK = 256, 896, 256
HALF = RANK // 2
PIECE = TOK // NM
CHUNK = COLS // 8
NEAR = (0, 1, -1, -2)
REACH = (4, 12, 3, 13, 2, 14, 1, 15)
PEERS = ((2, 1), (1, 1), (3, 1), (2, 0), (0, 1), (1, 0), (3, 0))
NEAR_FIRST = (0, 1, 7, 2, 6, 3, 5, 4)


def kernel(
    factor,
    a_hbm, g_hbm, p_hbm,
    c_out,
    a, at, g, p,
    pz, p2, pfull, part, rs, red,
    cown, csend, crecv, sb, rs2, far, cres,
    in_sem,
    p1s, p1f, p1r, p2s, p2r, p3s, p3r,
    r1s, r1r, r2s, r2r,
    d1s, d1r, d2s, d2r, d3s, d3r, d4s, d4r, d5s, d5r,
):
    dp, m = lax.axis_index("dp"), lax.axis_index("mp")
    z, yl, core = dp // 4, (dp // 2) % 2, dp % 2
    sign = 1 - 2 * core

    def dev(z_, yl_, core_, m_):
        return ((z_ * 2 + yl_) * 2 + core_, m_)

    sibling = dev(z, yl, 1 - core, m)

    def remote(src, dst, ssem, rsem, to):
        return pltpu.make_async_remote_copy(
            src_ref=src, dst_ref=dst, send_sem=ssem, recv_sem=rsem, device_id=to, device_id_type=MESH
        )

    def arrived(dst, rsem):
        remote(dst, dst, rsem, rsem, sibling).wait_recv()

    sent = []

    def send(src, dst, ssem, rsem, to):
        copy = remote(src, dst, ssem, rsem, to)
        copy.start()
        return copy

    loads = [
        pltpu.make_async_copy(src, dst, in_sem.at[i])
        for i, (src, dst) in enumerate(
            ((p_hbm, p), (a_hbm, a), (g_hbm, g))
        )
    ]
    for load in loads:
        load.start()

    barrier = pltpu.get_barrier_semaphore()

    def greet(to):
        pl.semaphore_signal(barrier, inc=1, device_id=to, device_id_type=MESH)

    for k in REACH:
        greet(dev((z + k) % NZ, yl, core, m))
    for k in range(1, NM):
        greet(dev(z, yl, core, (m + k) % NM))
    for k in range(NM):
        greet(dev(z, 1 - yl, core, (m + k) % NM))
    for k in (2, 14, 1, 15):
        greet(dev((z + k) % NZ, 1 - yl, core, m))
    greet(sibling)
    loads[0].wait()
    pl.semaphore_wait(barrier, 8 + 7 + 8 + 4 + 1)

    slot = jnp.minimum(m, SLICES - 1)
    cut = pl.ds(pl.multiple_of(slot * SL, SL), SL)

    def along(k):
        return remote(p.at[cut], pz.at[z], p1s.at[k], p1r.at[z], dev((z + k) % NZ, yl, core, m))

    @pl.when(m < SLICES)
    def _():
        for k in REACH:
            along(k).start()
        pz[z] = p[cut]

    loads[1].wait()
    for k in range(COLS // 128):
        at[128 * k : 128 * (k + 1)] = a[:, 128 * k : 128 * (k + 1)].T

    @pl.when(m < SLICES)
    def _():
        for way, steps in ((sign, (4, 3, 2, 1)), (-sign, (3, 2, 1))):
            source = (z - 4 * way + NZ) % NZ
            arrived(pz.at[source], p1r.at[source])
            for k in steps:
                remote(
                    pz.at[source], pz.at[source], p1f.at[way * sign + 1, k], p1r.at[source],
                    dev((z + way * k + NZ) % NZ, yl, core, m),
                ).start()
        for q in NEAR_FIRST:
            mt = (z // 2 + q) % NM
            for s in range(2):
                zs = 2 * mt + s
                gone = (zs - z + NZ) % NZ

                @pl.when((gone != 0) & (gone != 4) & (gone != NZ - 4))
                def _():
                    arrived(pz.at[zs], p1r.at[zs])

            src = pz.at[pl.ds(2 * mt, 2)]
            remote(src, p2.at[core, yl, slot], p2s.at[q], p2r.at[yl, slot], dev(z, 1 - yl, core, mt)).start()

            @pl.when(mt != m)
            def _():
                remote(src, p2.at[core, yl, slot], p2s.at[NM + q], p2r.at[yl, slot], dev(z, yl, core, mt)).start()

            @pl.when(mt == m)
            def _():
                p2[core, yl, slot] = pz[pl.ds(2 * mt, 2)]

    for ms in range(SLICES):
        for ys in range(2):
            @pl.when((ms != m) | (ys != yl))
            def _():
                arrived(p2.at[core, ys, ms], p2r.at[ys, ms])

            sent.append(send(p2.at[core, ys, ms], p2.at[core, ys, ms], p3s.at[ys, ms], p3r.at[ys, ms], sibling))
    for ms in range(SLICES):
        for ys in range(2):
            arrived(p2.at[1 - core, ys, ms], p3r.at[ys, ms])
    for c in range(2):
        for ys in range(2):
            for ms in range(SLICES):
                for s in range(2):
                    at_row = BLK * (4 * s + 2 * ys + c) + SL * ms
                    pfull[at_row : at_row + SL] = p2[c, ys, ms, s]

    loads[2].wait()
    part[...] = jnp.dot(g[...], pfull[...], preferred_element_type=F32).astype(BF16)

    def piece(i):
        return pl.ds(pl.multiple_of(i * PIECE, PIECE), PIECE)

    peers = [((m // 2 + dx) % 4) * 2 + (m + dh) % 2 for dx, dh in PEERS]
    for k, mt in enumerate(peers):
        sent.append(send(part.at[piece(mt)], rs.at[m], r1s.at[k], r1r.at[m], dev(z, yl, core, mt)))
    rs[m] = part[piece(m)]
    for mt in peers:
        arrived(rs.at[mt], r1r.at[mt])
    total = rs[0].astype(F32)
    for i in range(1, NM):
        total += rs[i].astype(F32)
    red[piece(m)] = total.astype(BF16)
    for k, mt in enumerate(peers):
        sent.append(send(red.at[piece(m)], red.at[piece(m)], r2s.at[k], r2r.at[m], dev(z, yl, core, mt)))
    for mt in peers:
        arrived(red.at[piece(mt)], r2r.at[mt])

    def chunk(z_, yl_):
        return pl.ds(pl.multiple_of((2 * (z_ % 4) + yl_) * CHUNK, SL), CHUNK)

    order = (
        (3, (z - 2 * sign + NZ) % NZ),
        (1 + core, (z + 1) % NZ),
        (2 - core, (z + NZ - 1) % NZ),
        (0, z),
    )
    for j, (_, zo) in enumerate(order):
        for other in (1, 0):
            rows = chunk(zo, (yl + other) % 2)
            tile = jnp.dot(at[rows], red[...], preferred_element_type=F32)
            low, high = tile[:, :HALF], tile[:, HALF:]
            cown[rows] = jnp.where(core == 0, low, high)
            csend[rows] = jnp.where(core == 0, high, low).astype(BF16)
            sent.append(send(csend.at[rows], crecv.at[rows], d1s.at[j, other], d1r.at[j, other], sibling))
    for j, (i, zo) in enumerate(order):
        for other in (1, 0):
            yo = (yl + other) % 2
            rows = chunk(zo, yo)
            arrived(crecv.at[rows], d1r.at[j, other])
            sb[rows] = (cown[rows] + crecv[rows].astype(F32)).astype(BF16)
            if j < 3 or other == 1:
                sent.append(send(sb.at[rows], rs2.at[i, yl], d2s.at[j, other], d2r.at[i, yl], dev(zo, yo, core, m)))
    rs2[0, yl] = sb[chunk(z, yl)]
    arrived(rs2.at[0, 1 - yl], d2r.at[0, 1 - yl])
    for i in (1, 2, 3):
        for y in range(2):
            arrived(rs2.at[i, y], d2r.at[i, y])
    total = rs2[0, 0].astype(F32) + rs2[0, 1].astype(F32)
    for i in (1, 2, 3):
        total += rs2[i, 0].astype(F32) + rs2[i, 1].astype(F32)
    zh = z // 4
    far[zh] = total.astype(BF16)
    for k in (2, 1, 3):
        sent.append(send(far.at[zh], far.at[zh], d3s.at[k], d3r.at[zh], dev((z + 4 * k) % NZ, yl, core, m)))
    for k in (1, 3, 2):
        arrived(far.at[(zh + k) % 4], d3r.at[(zh + k) % 4])
    total = far[0].astype(F32)
    for i in range(1, 4):
        total += far[i].astype(F32)
    own = chunk(z, yl)
    cres[core, own] = (total * factor).astype(BF16)
    for i in (3, 1, 2, 0):
        zu = (z - sign * NEAR[i] + NZ) % NZ
        for other in (1, 0):
            if i == 0 and other == 0:
                continue
            yu = (yl + other) % 2
            sent.append(
                send(cres.at[core, own], cres.at[core, own], d4s.at[i, other], d4r.at[i, yl], dev(zu, yu, core, m))
            )
    sent.append(send(cres.at[core, own], cres.at[core, own], d5s.at[0, 0], d5r.at[0, 0], sibling))
    for i in (0, 1, 2, 3):
        zo = (z + sign * NEAR[i] + NZ) % NZ
        for other in (0, 1):
            if i == 0 and other == 0:
                continue
            yo = (yl + other) % 2
            place = cres.at[core, chunk(zo, yo)]
            arrived(place, d4r.at[i, yo])
            sent.append(send(place, place, d5s.at[i, other], d5r.at[i, other], sibling))
    for i in (0, 1, 2, 3):
        zo = (z - sign * NEAR[i] + NZ) % NZ
        for other in (0, 1):
            arrived(cres.at[1 - core, chunk(zo, (yl + other) % 2)], d5r.at[i, other])

    for k in range(COLS // 128):
        rows = slice(128 * k, 128 * (k + 1))
        c_out[rows, :HALF] = cres[0, rows]
        c_out[rows, HALF:] = cres[1, rows]

    @pl.when(m < SLICES)
    def _():
        for k in REACH:
            along(k).wait_send()
        for way, steps in ((sign, (4, 3, 2, 1)), (-sign, (3, 2, 1))):
            source = (z - 4 * way + NZ) % NZ
            for k in steps:
                remote(pz.at[source], pz.at[source], p1f.at[way * sign + 1, k], p1r.at[source], sibling).wait_send()
        for q in NEAR_FIRST:
            mt = (z // 2 + q) % NM
            src = pz.at[pl.ds(2 * mt, 2)]
            remote(src, p2.at[core, yl, slot], p2s.at[q], p2r.at[yl, slot], sibling).wait_send()

            @pl.when(mt != m)
            def _():
                remote(src, p2.at[core, yl, slot], p2s.at[NM + q], p2r.at[yl, slot], sibling).wait_send()

    for copy in sent:
        copy.wait_send()


def step(m_ref, c_ref, p_ref, w_ref, m_out, w_out, mom, sem):
    copies = []
    for k in range(COLS // 128):
        rows = slice(128 * k, 128 * (k + 1))
        new = 0.9 * m_ref[rows] + c_ref[rows].astype(F32)
        mom[rows] = new
        copies.append(pltpu.make_async_copy(mom.at[rows], m_out.at[rows], sem.at[k]))
        copies[-1].start()
        update = lax.dot_general(p_ref[...], new.astype(BF16), (((1,), (1,)), ((), ())), preferred_element_type=F32)
        w_out[:, rows] = (w_ref[:, rows].astype(F32) - 2.0 * update).astype(BF16)
    for copy in copies:
        copy.wait()


def shards(attn_out, out_grad, projection, momentum, weight):
    factor = 1.0 / math.sqrt(attn_out.shape[0] * lax.axis_size("dp"))
    vmem, dma = pltpu.VMEM, pltpu.SemaphoreType.DMA
    compressed = pl.pallas_call(
        functools.partial(kernel, factor),
        out_shape=jax.ShapeDtypeStruct((COLS, RANK), BF16),
        in_specs=[pl.BlockSpec(memory_space=pltpu.HBM)] * 3,
        out_specs=pl.BlockSpec(memory_space=vmem),
        scratch_shapes=[
            vmem((TOK, COLS), BF16), vmem((COLS, TOK), BF16), vmem((TOK, COLS), BF16),
            vmem((BLK, RANK), BF16),
            vmem((NZ, SL, RANK), BF16), vmem((2, 2, SLICES, 2, SL, RANK), BF16), vmem((COLS, RANK), BF16),
            vmem((TOK, RANK), BF16), vmem((NM, PIECE, RANK), BF16), vmem((TOK, RANK), BF16),
            vmem((COLS, HALF), F32), vmem((COLS, HALF), BF16), vmem((COLS, HALF), BF16),
            vmem((COLS, HALF), BF16), vmem((4, 2, CHUNK, HALF), BF16), vmem((4, CHUNK, HALF), BF16),
            vmem((2, COLS, HALF), BF16),
            dma((3,)),
            dma((NZ,)), dma((3, 5)), dma((NZ,)), dma((2 * NM,)), dma((2, SLICES)), dma((2, SLICES)), dma((2, SLICES)),
            dma((NM,)), dma((NM,)), dma((NM,)), dma((NM,)),
            dma((4, 2)), dma((4, 2)), dma((4, 2)), dma((4, 2)), dma((4,)), dma((4,)),
            dma((4, 2)), dma((4, 2)), dma((4, 2)), dma((4, 2)),
        ],
        compiler_params=pltpu.CompilerParams(
            collective_id=0, has_side_effects=True, vmem_limit_bytes=213 * 2**18
        ),
        cost_estimate=pl.CostEstimate(flops=300_000_000, bytes_accessed=4_000_000, transcendentals=0),
        name="compress",
    )(attn_out, out_grad, projection)
    new_momentum, new_weight = pl.pallas_call(
        step,
        out_shape=(
            jax.ShapeDtypeStruct((COLS, RANK), F32),
            jax.ShapeDtypeStruct((BLK, COLS), BF16),
        ),
        in_specs=[pl.BlockSpec(memory_space=vmem)] * 4,
        out_specs=(pl.BlockSpec(memory_space=pltpu.HBM), pl.BlockSpec(memory_space=vmem)),
        scratch_shapes=[vmem((COLS, RANK), F32), dma((COLS // 128,))],
        compiler_params=pltpu.CompilerParams(vmem_limit_bytes=16 * 2**20),
        cost_estimate=pl.CostEstimate(flops=51_000_000, bytes_accessed=3_000_000, transcendentals=0),
        name="momentum_and_weight",
    )(momentum, compressed, projection, weight.T)
    return (new_momentum, new_weight.T)


def solution(mesh):
    return jax.shard_map(
        shards,
        mesh=mesh,
        in_specs=(P("dp", "mp"), P("dp", "mp"), P("dp", None), P("mp", None), P("mp", "dp")),
        out_specs=(P("mp", None), P("mp", "dp")),
        check_vma=False,
    )
```

time: 75.1 us -> 67.5 us (0.90)
  local copies, waits for them, and re-layouts: 5.15 us -> 0.9 us
  Pallas kernels: 68 us -> 65.8 us
  other arithmetic: 1.02 us -> 0 us
    unnamed x12 -> x6, local copies, waits for them, and re-layouts: 5.15 us -> 0.9 us
    pallas_call x1 -> x2, Pallas kernels: 68 us -> 65.8 us  [the longest x1 64 us: shards(): pl.pallas_call(functools.partial(kernel, factor), out_shape=jax.ShapeDtyp...]
    add x1 -> x0, other arithmetic: 1.02 us -> none  [shards(): new_momentum = 0.9 * momentum + compressed.astype(F32)]
where the time goes in v3:
time: 67.5 us; the launch traced here: 67.4 us
  Pallas kernels  65.8 us (97%)
  local copies, waits for them, and re-layouts  0.9 us (1%)
    pallas_call x1, Pallas kernels, shards(): pl.pallas_call(functools.partial(kernel, factor), out_shape=jax.ShapeDtyp...  64 us
    pallas_call x1, Pallas kernels, shards(): pl.pallas_call(step, out_shape=(jax.ShapeDtypeStruct((COLS, RANK), F32),...  1.83 us

profile of v3, /device:TPU:1, one launch (start us, length us, event | category | flops | bytes accessed | tf_op | source)
XLA Modules:
  0.0 67.4 jit_solution(12798353493960250592)
XLA Ops:
  0.6 0.0 copy-start
  0.6 0.0 copy-start.1
  0.7 0.9 %copy-done.1 = bf16[112,256]{1,0:T(8,128)(2,1)S(1)} copy-done((bf16[112,256]{1,0:T(8,128)(2,1)S(1)}, bf16[112,256]{1,0:T(8,128)(2,1)}, u32[]{:S(2)}) %copy-start.1) | copy-done | bytes 57368
  1.5 0.0 copy-start.2
  1.5 64.0 %compress.1.c_ref = bf16[896,256]{1,0:T(8,128)(2,1)S(1)} custom-call(bf16[256,896]{1,0:T(8,128)(2,1)} %a_hbm.1, bf16[256,896]{1,0:T(8,128)(2,1)} %g_hbm.1, bf16[112,256]{1,0:T(8,128)(2,1)S(1)} %copy-done.1), custom_call_target="tpu_custom_call" | custom-call | flops 300000000 | bytes 4000000 | tf_op jit(solution)/shard_map/compress/pallas_call | solution.py:287
  65.5 0.0 copy-done
  65.5 0.0 copy-done.2
  65.5 1.8 %momentum_and_weight.1 = (f32[896,256]{1,0:T(8,128)}, bf16[112,896]{1,0:T(8,128)(2,1)}) custom-call(f32[896,256]{1,0:T(8,128)S(1)} %copy-done, bf16[896,256]{1,0:T(8,128)(2,1)S(1)} %compress.1.c_ref, bf16[112,256]{1,0:T(8,128)(2,1)S(1)} %copy-done.1, bf16[112,896]{1,0:T(8,128)(2,1)S(1)} %bitcast.2), custom_call_target="tpu_custom_call" | custom-call | flops 51000000 | bytes 3000000 | tf_op jit(solution)/shard_map/momentum_and_weight/pallas_call | solution.py:312
Async XLA Ops:
  0.6 64.9 %copy-start = (f32[896,256]{1,0:T(8,128)S(1)}, f32[896,256]{1,0:T(8,128)}, u32[]{:S(2)}) copy-start(f32[896,256]{1,0:T(8,128)} %m_ref.1) | copy-start | bytes 2752516
  0.6 0.9 %copy-start.1 = (bf16[112,256]{1,0:T(8,128)(2,1)S(1)}, bf16[112,256]{1,0:T(8,128)(2,1)}, u32[]{:S(2)}) copy-start(bf16[112,256]{1,0:T(8,128)(2,1)} %p_ref.1) | copy-start | bytes 172036
  1.5 64.0 %copy-start.2 = (bf16[896,112]{0,1:T(8,128)(2,1)S(1)}, bf16[896,112]{0,1:T(8,128)(2,1)}, u32[]{:S(2)}) copy-start(bf16[896,112]{0,1:T(8,128)(2,1)} %param.9) | copy-start | bytes 602116

commit v4 on v3

v4 whole, which is shorter than its diff:
```python
import functools
import math

import jax
import jax.numpy as jnp
from jax import lax
from jax.experimental import pallas as pl
from jax.experimental.pallas import tpu as pltpu
from jax.sharding import PartitionSpec as P

MESH = pl.DeviceIdType.MESH
BF16 = jnp.bfloat16
F32 = jnp.float32

NZ, NM = 16, 8
BLK = 112
SL = 16
SLICES = 7
TOK, COLS, RANK = 256, 896, 256
HALF = RANK // 2
PIECE = TOK // NM
CHUNK = COLS // 8
NEAR = (0, 1, -1, -2)
REACH = (4, 12, 3, 13, 2, 14, 1, 15)
PEERS = ((2, 1), (1, 1), (3, 1), (2, 0), (0, 1), (1, 0), (3, 0))
SCATTER = tuple((dy, mt) for dy in (1, 0) for mt in (0, 1, 2, 3, 4, 5, 6, None) if dy or mt is not None)
SUBS = ((0, 112),)


def kernel(
    factor,
    a_hbm, g_hbm, p_hbm,
    c_out,
    a, at, g, p,
    gs, gq, pz, mine, part, rs, rsum, red,
    sb, rs2, far, cres,
    in_sem,
    p1s, p1f, p1r, gss, gsr, xs, xr, a_s, a_r,
    r1s, r1r, r2s, r2r,
    d2s, d2r, d3s, d3r, d4s, d4r, d5s, d5r,
):
    dp, m = lax.axis_index("dp"), lax.axis_index("mp")
    z, yl, core = dp // 4, (dp // 2) % 2, dp % 2
    sign = 1 - 2 * core

    def dev(z_, yl_, core_, m_):
        return ((z_ * 2 + yl_) * 2 + core_, m_)

    sibling = dev(z, yl, 1 - core, m)

    def remote(src, dst, ssem, rsem, to):
        return pltpu.make_async_remote_copy(
            src_ref=src, dst_ref=dst, send_sem=ssem, recv_sem=rsem, device_id=to, device_id_type=MESH
        )

    def arrived(dst, rsem):
        remote(dst, dst, rsem, rsem, sibling).wait_recv()

    sent = []

    def send(src, dst, ssem, rsem, to):
        copy = remote(src, dst, ssem, rsem, to)
        copy.start()
        sent.append(copy)

    loads = [
        pltpu.make_async_copy(src, dst, in_sem.at[i])
        for i, (src, dst) in enumerate(((p_hbm, p), (g_hbm, g), (a_hbm, a)))
    ]
    for load in loads:
        load.start()

    peers = [((m // 2 + dx) % 4) * 2 + (m + dh) % 2 for dx, dh in PEERS]
    plane = [(mt, (yl + dy) % 2) for mt in peers for dy in (1, 0)] + [(m, 1 - yl)]

    barrier = pltpu.get_barrier_semaphore()

    def greet(to):
        pl.semaphore_signal(barrier, inc=1, device_id=to, device_id_type=MESH)

    for k in REACH:
        greet(dev((z + k) % NZ, yl, core, m))
    for mt, yt in plane:
        greet(dev(z, yt, core, mt))
    greet(sibling)
    loads[0].wait()
    pl.semaphore_wait(barrier, 8 + 15 + 1)

    slot = jnp.minimum(m, SLICES - 1)
    cut = pl.ds(pl.multiple_of(slot * SL, SL), SL)

    def along(k):
        return remote(p.at[cut], pz.at[core, z], p1s.at[k], p1r.at[z], dev((z + k) % NZ, yl, core, m))

    def onward(way, k):
        source = (z - 4 * way + NZ) % NZ
        return remote(
            pz.at[core, source], pz.at[core, source], p1f.at[way * sign + 1, k], p1r.at[source],
            dev((z + way * k + NZ) % NZ, yl, core, m),
        )

    def twin(source):
        return remote(pz.at[core, source], pz.at[core, source], xs.at[source], xr.at[source], sibling)

    ways = ((sign, (4, 3, 2, 1)), (-sign, (3, 2, 1)))

    @pl.when(m < SLICES)
    def _():
        for k in REACH:
            along(k).start()
        pz[core, z] = p[cut]
        twin(z).start()

    loads[1].wait()
    for k in range(COLS // 128):
        tile = g[:, 128 * k : 128 * (k + 1)].T
        for i in range(128 // SL):
            group = k * (128 // SL) + i
            block, ms = group // SLICES, group % SLICES
            gs[(block // 2) % 2, ms, block % 2, block // 4] = tile[SL * i : SL * (i + 1)]

    def spread(j):
        mt, yt = plane[j]
        mt = jnp.minimum(mt, SLICES - 1)
        return remote(gs.at[yt, mt], gq.at[yl, m], gss.at[j], gsr.at[yl, m], dev(z, yt, core, mt))

    for j, (mt, _) in enumerate(plane):
        @pl.when(mt < SLICES)
        def _():
            spread(j).start()

    @pl.when(m < SLICES)
    def _():
        gq[yl, m] = gs[yl, slot]
        for way, steps in ways:
            source = (z - 4 * way + NZ) % NZ
            arrived(pz.at[core, source], p1r.at[source])
            for k in steps:
                onward(way, k).start()
            twin(source).start()

    loads[2].wait()
    for k in range(COLS // 128):
        at[core, 128 * k : 128 * (k + 1)] = a[:, 128 * k : 128 * (k + 1)].T
    send(at.at[core], at.at[core], a_s, a_r, sibling)

    def piece(i):
        return pl.ds(pl.multiple_of(i * PIECE, PIECE), PIECE)

    def scatter(j):
        yt, mt = SCATTER[j][0], SCATTER[j][1]
        yt = (yl + yt) % 2
        mt = m if mt is None else peers[mt]
        return remote(part.at[yt, piece(mt)], rs.at[yl, slot], r1s.at[j], r1r.at[yl, slot], dev(z, yt, core, mt))

    @pl.when(m < SLICES)
    def _():
        for k in (1, 15, 2, 14, 3, 13, 5, 11, 6, 10, 7, 9, 8):
            source = (z + k) % NZ
            arrived(pz.at[core, source], p1r.at[source])
            twin(source).start()
        for mt, yt in reversed(plane):
            arrived(gq.at[yt, mt], gsr.at[yt, mt])
        turned = pz[core].reshape(NZ * SL, RANK).T
        for yt in range(2):
            there = gq[yt, :, core].reshape(NZ * SL, TOK)
            mine[yt] = jnp.dot(turned, there, preferred_element_type=F32)
        for k in range(NZ):
            arrived(pz.at[1 - core, k], xr.at[k])
        turned = pz[1 - core].reshape(NZ * SL, RANK).T
        for dy in (1, 0):
            yt = (yl + dy) % 2
            there = gq[yt, :, 1 - core].reshape(NZ * SL, TOK)
            part[yt] = (mine[yt] + jnp.dot(turned, there, preferred_element_type=F32)).astype(BF16)
            for j, (step_y, _) in enumerate(SCATTER):
                if step_y == dy:
                    scatter(j).start()
        rs[yl, slot] = part[yl, piece(m)]

    for ms in range(SLICES):
        for ys in range(2):
            @pl.when((ms != m) | (ys != yl))
            def _():
                arrived(rs.at[ys, ms], r1r.at[ys, ms])

    total = rs[0, 0].astype(F32) + rs[1, 0].astype(F32)
    for ms in range(1, SLICES):
        total += rs[0, ms].astype(F32) + rs[1, ms].astype(F32)
    rsum[...] = total.astype(BF16)
    arrived(at.at[1 - core], a_r)
    half = m // 4
    place = red.at[core, piece(m % 4)]
    for k, mt in enumerate(peers):
        send(rsum, place, r2s.at[k], r2r.at[core, m % 4], dev(z, yl, half, mt))

    def across():
        return remote(rsum, place, r2s.at[7], r2r.at[core, m % 4], sibling)

    @pl.when(half != core)
    def _():
        across().start()

    @pl.when(half == core)
    def _():
        red[core, piece(m % 4)] = rsum[...]

    for c in range(2):
        for q in range(4):
            @pl.when((c != core) | (4 * core + q != m))
            def _():
                arrived(red.at[c, piece(q)], r2r.at[c, q])

    def chunk(z_, yl_, sub=(0, CHUNK)):
        return pl.ds(pl.multiple_of((2 * (z_ % 4) + yl_) * CHUNK + sub[0], SL), sub[1])

    order = (
        (3, (z - 2 * sign + NZ) % NZ),
        (1 + core, (z + 1) % NZ),
        (2 - core, (z + NZ - 1) % NZ),
        (0, z),
    )
    turned = [red[c].T for c in range(2)]

    def to_owner(b, j, dy):
        i, zo = order[j]
        yo = (yl + dy) % 2
        send(
            sb.at[chunk(zo, yo, SUBS[b])], rs2.at[i, yl, pl.ds(*SUBS[b])], d2s.at[b, j, dy], d2r.at[b, i, yl],
            dev(zo, yo, core, m),
        )

    for j, (_, zo) in enumerate(order):
        for dy in (1, 0):
            rows = chunk(zo, (yl + dy) % 2)
            tile = jnp.dot(at[0, rows], turned[0], preferred_element_type=F32)
            sb[rows] = (tile + jnp.dot(at[1, rows], turned[1], preferred_element_type=F32)).astype(BF16)
            if j < 3 or dy == 1:
                to_owner(0, j, dy)
    for b in range(1, len(SUBS)):
        for j in range(4):
            for dy in (1, 0):
                if j < 3 or dy == 1:
                    to_owner(b, j, dy)
    for sub in SUBS:
        part_rows = pl.ds(*sub)
        rs2[0, yl, part_rows] = sb[chunk(z, yl, sub)]
    zh = z // 4
    for b, sub in enumerate(SUBS):
        part_rows = pl.ds(*sub)
        place = rs2.at[0, 1 - yl, part_rows]
        arrived(place, d2r.at[b, 0, 1 - yl])
        for i in (1, 2, 3):
            for y in range(2):
                arrived(rs2.at[i, y, part_rows], d2r.at[b, i, y])
        total = rs2[0, 0, part_rows].astype(F32) + rs2[0, 1, part_rows].astype(F32)
        for i in (1, 2, 3):
            total += rs2[i, 0, part_rows].astype(F32) + rs2[i, 1, part_rows].astype(F32)
        far[zh, part_rows] = total.astype(BF16)
        for k in (2, 1, 3):
            place = far.at[zh, part_rows]
            send(place, place, d3s.at[b, k], d3r.at[b, zh], dev((z + 4 * k) % NZ, yl, core, m))
    for b, sub in enumerate(SUBS):
        part_rows = pl.ds(*sub)
        for k in (1, 3, 2):
            arrived(far.at[(zh + k) % 4, part_rows], d3r.at[b, (zh + k) % 4])
        total = far[0, part_rows].astype(F32)
        for i in range(1, 4):
            total += far[i, part_rows].astype(F32)
        own = chunk(z, yl, sub)
        cres[core, own] = (total * factor).astype(BF16)
        place = cres.at[core, own]
        for i in (3, 1, 2, 0):
            zu = (z - sign * NEAR[i] + NZ) % NZ
            for dy in (1, 0):
                if i > 0 or dy == 1:
                    yu = (yl + dy) % 2
                    send(place, place, d4s.at[b, i, dy], d4r.at[b, i, yl], dev(zu, yu, core, m))
        send(place, place, d5s.at[b, 0, 0], d5r.at[b, 0, 0], sibling)
    for b, sub in enumerate(SUBS):
        for i in (0, 1, 2, 3):
            zo = (z + sign * NEAR[i] + NZ) % NZ
            for dy in (0, 1):
                if i > 0 or dy == 1:
                    yo = (yl + dy) % 2
                    place = cres.at[core, chunk(zo, yo, sub)]
                    arrived(place, d4r.at[b, i, yo])
                    send(place, place, d5s.at[b, i, dy], d5r.at[b, i, dy], sibling)
    for b, sub in enumerate(SUBS):
        for i in (0, 1, 2, 3):
            zo = (z - sign * NEAR[i] + NZ) % NZ
            for dy in (0, 1):
                arrived(cres.at[1 - core, chunk(zo, (yl + dy) % 2, sub)], d5r.at[b, i, dy])

    for k in range(COLS // 128):
        rows = slice(128 * k, 128 * (k + 1))
        c_out[rows, :HALF] = cres[0, rows]
        c_out[rows, HALF:] = cres[1, rows]

    for j, (mt, _) in enumerate(plane):
        @pl.when(mt < SLICES)
        def _():
            spread(j).wait_send()

    @pl.when(half != core)
    def _():
        across().wait_send()

    @pl.when(m < SLICES)
    def _():
        for k in REACH:
            along(k).wait_send()
        for way, steps in ways:
            for k in steps:
                onward(way, k).wait_send()
        for k in range(NZ):
            twin(k).wait_send()
        for j in range(len(SCATTER)):
            scatter(j).wait_send()

    for copy in sent:
        copy.wait_send()


def step(m_ref, c_ref, p_ref, w_ref, m_out, w_out, mom, sem):
    copies = []
    for k in range(COLS // 128):
        rows = slice(128 * k, 128 * (k + 1))
        new = 0.9 * m_ref[rows] + c_ref[rows].astype(F32)
        mom[rows] = new
        copies.append(pltpu.make_async_copy(mom.at[rows], m_out.at[rows], sem.at[k]))
        copies[-1].start()
        update = lax.dot_general(p_ref[...], new.astype(BF16), (((1,), (1,)), ((), ())), preferred_element_type=F32)
        w_out[:, rows] = (w_ref[:, rows].astype(F32) - 2.0 * update).astype(BF16)
    for copy in copies:
        copy.wait()


def shards(attn_out, out_grad, projection, momentum, weight):
    factor = 1.0 / math.sqrt(attn_out.shape[0] * lax.axis_size("dp"))
    vmem, dma = pltpu.VMEM, pltpu.SemaphoreType.DMA
    compressed = pl.pallas_call(
        functools.partial(kernel, factor),
        out_shape=jax.ShapeDtypeStruct((COLS, RANK), BF16),
        in_specs=[pl.BlockSpec(memory_space=pltpu.HBM)] * 3,
        out_specs=pl.BlockSpec(memory_space=vmem),
        scratch_shapes=[
            vmem((TOK, COLS), BF16), vmem((2, COLS, TOK), BF16), vmem((TOK, COLS), BF16), vmem((BLK, RANK), BF16),
            vmem((2, SLICES, 2, 2, SL, TOK), BF16), vmem((2, NM, 2, 2, SL, TOK), BF16), vmem((2, NZ, SL, RANK), BF16),
            vmem((2, RANK, TOK), F32), vmem((2, RANK, TOK), BF16), vmem((2, SLICES, PIECE, TOK), BF16),
            vmem((PIECE, TOK), BF16), vmem((2, HALF, TOK), BF16),
            vmem((COLS, HALF), BF16), vmem((4, 2, CHUNK, HALF), BF16), vmem((4, CHUNK, HALF), BF16),
            vmem((2, COLS, HALF), BF16),
            dma((3,)),
            dma((NZ,)), dma((3, 5)), dma((NZ,)), dma((15,)), dma((2, NM)), dma((NZ,)), dma((NZ,)), dma, dma,
            dma((15,)), dma((2, SLICES)), dma((NM,)), dma((2, 4)),
            dma((2, 4, 2)), dma((2, 4, 2)), dma((2, 4)), dma((2, 4)),
            dma((2, 4, 2)), dma((2, 4, 2)), dma((2, 4, 2)), dma((2, 4, 2)),
        ],
        compiler_params=pltpu.CompilerParams(
            collective_id=0, has_side_effects=True, vmem_limit_bytes=213 * 2**18
        ),
        cost_estimate=pl.CostEstimate(flops=300_000_000, bytes_accessed=4_000_000, transcendentals=0),
        name="compress",
    )(attn_out, out_grad, projection)
    new_momentum, new_weight = pl.pallas_call(
        step,
        out_shape=(
            jax.ShapeDtypeStruct((COLS, RANK), F32),
            jax.ShapeDtypeStruct((BLK, COLS), BF16),
        ),
        in_specs=[pl.BlockSpec(memory_space=vmem)] * 4,
        out_specs=(pl.BlockSpec(memory_space=pltpu.HBM), pl.BlockSpec(memory_space=vmem)),
        scratch_shapes=[vmem((COLS, RANK), F32), dma((COLS // 128,))],
        compiler_params=pltpu.CompilerParams(vmem_limit_bytes=16 * 2**20),
        cost_estimate=pl.CostEstimate(flops=51_000_000, bytes_accessed=3_000_000, transcendentals=0),
        name="momentum_and_weight",
    )(momentum, compressed, projection, weight.T)
    return (new_momentum, new_weight.T)


def solution(mesh):
    return jax.shard_map(
        shards,
        mesh=mesh,
        in_specs=(P("dp", "mp"), P("dp", "mp"), P("dp", None), P("mp", None), P("mp", "dp")),
        out_specs=(P("mp", None), P("mp", "dp")),
        check_vma=False,
    )
```

time: 67.5 us -> 62.9 us (0.932)
  Pallas kernels: 65.8 us -> 61.2 us
    pallas_call x1, Pallas kernels: 64 us -> 59.4 us  [shards(): pl.pallas_call(functools.partial(kernel, factor), out_shape=jax.ShapeDtyp...]
where the time goes in v4:
time: 62.9 us; the launch traced here: 62.8 us
  Pallas kernels  61.2 us (97%)
  local copies, waits for them, and re-layouts  0.9 us (1%)
  between operations  0.67 us (1%)
    pallas_call x1, Pallas kernels, shards(): pl.pallas_call(functools.partial(kernel, factor), out_shape=jax.ShapeDtyp...  59.4 us
    pallas_call x1, Pallas kernels, shards(): pl.pallas_call(step, out_shape=(jax.ShapeDtypeStruct((COLS, RANK), F32),...  1.84 us

profile of v4, /device:TPU:1, one launch (start us, length us, event | category | flops | bytes accessed | tf_op | source)
XLA Modules:
  0.0 62.8 jit_solution(9660019796767475658)
XLA Ops:
  0.6 0.0 copy-start
  0.6 0.0 copy-start.1
  0.7 0.9 %copy-done.1 = bf16[112,256]{1,0:T(8,128)(2,1)S(1)} copy-done((bf16[112,256]{1,0:T(8,128)(2,1)S(1)}, bf16[112,256]{1,0:T(8,128)(2,1)}, u32[]{:S(2)}) %copy-start.1) | copy-done | bytes 57368
  1.5 0.0 copy-start.2
  1.5 59.4 %compress.1.c_ref = bf16[896,256]{1,0:T(8,128)(2,1)S(1)} custom-call(bf16[256,896]{1,0:T(8,128)(2,1)} %a_hbm.1, bf16[256,896]{1,0:T(8,128)(2,1)} %g_hbm.1, bf16[112,256]{1,0:T(8,128)(2,1)S(1)} %copy-done.1), custom_call_target="tpu_custom_call" | custom-call | flops 300000000 | bytes 4000000 | tf_op jit(solution)/shard_map/compress/pallas_call | solution.py:341
  60.9 0.0 copy-done
  60.9 0.0 copy-done.2
  61.0 1.8 %momentum_and_weight.1 = (f32[896,256]{1,0:T(8,128)}, bf16[112,896]{1,0:T(8,128)(2,1)}) custom-call(f32[896,256]{1,0:T(8,128)S(1)} %copy-done, bf16[896,256]{1,0:T(8,128)(2,1)S(1)} %compress.1.c_ref, bf16[112,256]{1,0:T(8,128)(2,1)S(1)} %copy-done.1, bf16[112,896]{1,0:T(8,128)(2,1)S(1)} %bitcast.2), custom_call_target="tpu_custom_call" | custom-call | flops 51000000 | bytes 3000000 | tf_op jit(solution)/shard_map/momentum_and_weight/pallas_call | solution.py:365
Async XLA Ops:
  0.6 60.3 %copy-start = (f32[896,256]{1,0:T(8,128)S(1)}, f32[896,256]{1,0:T(8,128)}, u32[]{:S(2)}) copy-start(f32[896,256]{1,0:T(8,128)} %m_ref.1) | copy-start | bytes 2752516
  0.6 0.9 %copy-start.1 = (bf16[112,256]{1,0:T(8,128)(2,1)S(1)}, bf16[112,256]{1,0:T(8,128)(2,1)}, u32[]{:S(2)}) copy-start(bf16[112,256]{1,0:T(8,128)(2,1)} %p_ref.1) | copy-start | bytes 172036
  1.5 59.4 %copy-start.2 = (bf16[896,112]{0,1:T(8,128)(2,1)S(1)}, bf16[896,112]{0,1:T(8,128)(2,1)}, u32[]{:S(2)}) copy-start(bf16[896,112]{0,1:T(8,128)(2,1)} %param.9) | copy-start | bytes 602116

commit v5 on v4

v5 whole, which is shorter than its diff:
```python
import functools
import math

import jax
import jax.numpy as jnp
from jax import lax
from jax.experimental import pallas as pl
from jax.experimental.pallas import tpu as pltpu
from jax.sharding import PartitionSpec as P

MESH = pl.DeviceIdType.MESH
BF16 = jnp.bfloat16
F32 = jnp.float32

NZ, NM = 16, 8
BLK = 112
SL = 16
SLICES = 7
TOK, COLS, RANK = 256, 896, 256
HALF = RANK // 2
PIECE = TOK // NM
CHUNKS = HALF // SL
NEAR = (0, 1, -1, -2)
REACH = (4, 12, 3, 13, 2, 14, 1, 15)
PEERS = ((2, 1), (1, 1), (3, 1), (2, 0), (0, 1), (1, 0), (3, 0))
SCATTER = tuple((dy, mt) for dy in (1, 0) for mt in (0, 1, 2, 3, 4, 5, 6, None) if dy or mt is not None)


def kernel(
    factor,
    a_hbm, g_hbm, p_hbm,
    cres,
    a, g, p,
    gs, gq, pz, mine, part, rs, rsum, red,
    sb, rs2, far,
    in_sem,
    p1s, p1f, p1r, gss, gsr, xs, xr, a_s, a_r,
    r1s, r1r, r2s, r2r,
    d2s, d2r, d3s, d3r, d4s, d4r, d5s, d5r,
):
    dp, m = lax.axis_index("dp"), lax.axis_index("mp")
    z, yl, core = dp // 4, (dp // 2) % 2, dp % 2
    sign = 1 - 2 * core

    def dev(z_, yl_, core_, m_):
        return ((z_ * 2 + yl_) * 2 + core_, m_)

    sibling = dev(z, yl, 1 - core, m)

    def remote(src, dst, ssem, rsem, to):
        return pltpu.make_async_remote_copy(
            src_ref=src, dst_ref=dst, send_sem=ssem, recv_sem=rsem, device_id=to, device_id_type=MESH
        )

    def arrived(dst, rsem):
        remote(dst, dst, rsem, rsem, sibling).wait_recv()

    sent = []

    def send(src, dst, ssem, rsem, to):
        copy = remote(src, dst, ssem, rsem, to)
        copy.start()
        sent.append(copy)

    loads = [
        pltpu.make_async_copy(src, dst, in_sem.at[i])
        for i, (src, dst) in enumerate(((p_hbm, p), (g_hbm, g), (a_hbm, a.at[core])))
    ]
    for load in loads:
        load.start()

    peers = [((m // 2 + dx) % 4) * 2 + (m + dh) % 2 for dx, dh in PEERS]
    plane = [(mt, (yl + dy) % 2) for mt in peers for dy in (1, 0)] + [(m, 1 - yl)]

    barrier = pltpu.get_barrier_semaphore()

    def greet(to):
        pl.semaphore_signal(barrier, inc=1, device_id=to, device_id_type=MESH)

    for k in REACH:
        greet(dev((z + k) % NZ, yl, core, m))
    for mt, yt in plane:
        greet(dev(z, yt, core, mt))
    greet(sibling)
    loads[1].wait()
    for k in range(COLS // 128):
        tile = g[:, 128 * k : 128 * (k + 1)].T
        for i in range(128 // SL):
            group = k * (128 // SL) + i
            block, ms = group // SLICES, group % SLICES
            gs[(block // 2) % 2, ms, block % 2, block // 4] = tile[SL * i : SL * (i + 1)]

    loads[0].wait()
    pl.semaphore_wait(barrier, 8 + 15 + 1)

    slot = jnp.minimum(m, SLICES - 1)
    cut = pl.ds(pl.multiple_of(slot * SL, SL), SL)

    def along(k):
        return remote(p.at[cut], pz.at[core, z], p1s.at[k], p1r.at[z], dev((z + k) % NZ, yl, core, m))

    def onward(way, k):
        source = (z - 4 * way + NZ) % NZ
        return remote(
            pz.at[core, source], pz.at[core, source], p1f.at[way * sign + 1, k], p1r.at[source],
            dev((z + way * k + NZ) % NZ, yl, core, m),
        )

    def twin(source):
        return remote(pz.at[core, source], pz.at[core, source], xs.at[source], xr.at[source], sibling)

    ways = ((sign, (4, 3, 2, 1)), (-sign, (3, 2, 1)))

    @pl.when(m < SLICES)
    def _():
        for k in REACH[:2]:
            along(k).start()
        pz[core, z] = p[cut]
        twin(z).start()

    def spread(j):
        mt, yt = plane[j]
        mt = jnp.minimum(mt, SLICES - 1)
        return remote(gs.at[yt, mt], gq.at[yl, m], gss.at[j], gsr.at[yl, m], dev(z, yt, core, mt))

    for j, (mt, _) in enumerate(plane):
        @pl.when(mt < SLICES)
        def _():
            spread(j).start()

    loads[2].wait()
    send(a.at[core], a.at[core], a_s, a_r, sibling)

    @pl.when(m < SLICES)
    def _():
        gq[yl, m] = gs[yl, slot]
        for way, steps in ways:
            source = (z - 4 * way + NZ) % NZ
            arrived(pz.at[core, source], p1r.at[source])
            for k in steps:
                onward(way, k).start()
            twin(source).start()
        for k in REACH[2:]:
            along(k).start()


    def piece(i):
        return pl.ds(pl.multiple_of(i * PIECE, PIECE), PIECE)

    def scatter(j):
        yt, mt = SCATTER[j][0], SCATTER[j][1]
        yt = (yl + yt) % 2
        mt = m if mt is None else peers[mt]
        return remote(part.at[yt, piece(mt)], rs.at[yl, slot], r1s.at[j], r1r.at[yl, slot], dev(z, yt, core, mt))

    @pl.when(m < SLICES)
    def _():
        for k in (1, 15, 2, 14, 3, 13, 5, 11, 6, 10, 7, 9, 8):
            source = (z + k) % NZ
            arrived(pz.at[core, source], p1r.at[source])
            twin(source).start()
        for mt, yt in reversed(plane):
            arrived(gq.at[yt, mt], gsr.at[yt, mt])
        turned = pz[core].reshape(NZ * SL, RANK).T
        for yt in range(2):
            there = gq[yt, :, core].reshape(NZ * SL, TOK)
            mine[yt] = jnp.dot(turned, there, preferred_element_type=F32)
        for k in range(NZ):
            arrived(pz.at[1 - core, k], xr.at[k])
        turned = pz[1 - core].reshape(NZ * SL, RANK).T
        for dy in (1, 0):
            yt = (yl + dy) % 2
            there = gq[yt, :, 1 - core].reshape(NZ * SL, TOK)
            part[yt] = (mine[yt] + jnp.dot(turned, there, preferred_element_type=F32)).astype(BF16)
            for j, (step_y, _) in enumerate(SCATTER):
                if step_y == dy:
                    scatter(j).start()
        rs[yl, slot] = part[yl, piece(m)]

    for ms in range(SLICES):
        for ys in range(2):
            @pl.when((ms != m) | (ys != yl))
            def _():
                arrived(rs.at[ys, ms], r1r.at[ys, ms])

    total = rs[0, 0].astype(F32) + rs[1, 0].astype(F32)
    for ms in range(1, SLICES):
        total += rs[0, ms].astype(F32) + rs[1, ms].astype(F32)
    rsum[...] = total.astype(BF16)
    def to_owner(q, dy):
        delta = (q - z + NZ) % 4
        zo = (z + jnp.where(delta == 2, -2 * sign, jnp.where(delta == 3, -1, delta)) + NZ) % NZ
        i = jnp.where(delta == 0, 0, jnp.where(delta == 2, 3, jnp.where((delta == 1) == (core == 0), 1, 2)))
        yo = (yl + dy) % 2
        return remote(sb.at[2 * q + yo], rs2.at[i, yl], d2s.at[q, dy], d2r.at[i, yl], dev(zo, yo, core, m))

    arrived(a.at[1 - core], a_r)
    half = m // 4
    place = red.at[core, piece(m % 4)]
    for k, mt in enumerate(peers):
        send(rsum, place, r2s.at[k], r2r.at[core, m % 4], dev(z, yl, half, mt))

    def across():
        return remote(rsum, place, r2s.at[7], r2r.at[core, m % 4], sibling)

    @pl.when(half != core)
    def _():
        across().start()

    @pl.when(half == core)
    def _():
        red[core, piece(m % 4)] = rsum[...]

    x, h = m // 2, m % 2
    near_x = jnp.where((x - 2 * core + 4) % 4 < 2, (x - 2 * core + 4) % 4, jnp.where((x - 2 * core + 4) % 4 == 2, 1, 0))
    for dh, dx in ((0, 0), (0, 1), (1, 0), (1, 1)):
        q = ((near_x + dx) % 2) * 2 + (h + dh) % 2
        for c in range(2):
            @pl.when((c != core) | (4 * core + q != m))
            def _():
                arrived(red.at[c, piece(q)], r2r.at[c, q])

        total = jnp.dot(red[0, piece(q)], a[0], preferred_element_type=F32)
        total += jnp.dot(red[1, piece(q)], a[1], preferred_element_type=F32)
        sb[2 * q] = total[:SL].astype(BF16)
        sb[2 * q + 1] = total[SL:].astype(BF16)
        for dy in (1, 0):
            @pl.when((dy == 1) | (q != z % 4))
            def _():
                to_owner(q, dy).start()

    rs2[0, yl] = sb[2 * (z % 4) + yl]
    zh = z // 4
    arrived(rs2.at[0, 1 - yl], d2r.at[0, 1 - yl])
    for i in (1, 2, 3):
        for y in range(2):
            arrived(rs2.at[i, y], d2r.at[i, y])
    total = rs2[0, 0].astype(F32) + rs2[0, 1].astype(F32)
    for i in (1, 2, 3):
        total += rs2[i, 0].astype(F32) + rs2[i, 1].astype(F32)
    far[zh] = total.astype(BF16)
    send(far.at[zh], far.at[zh], d3s.at[2], d3r.at[zh], dev((z + 8) % NZ, yl, core, m))

    for j, (mt, _) in enumerate(plane):
        @pl.when(mt < SLICES)
        def _():
            spread(j).wait_send()

    @pl.when(half != core)
    def _():
        across().wait_send()

    @pl.when(m < SLICES)
    def _():
        for k in REACH:
            along(k).wait_send()
        for way, steps in ways:
            for k in steps:
                onward(way, k).wait_send()
        for k in range(NZ):
            twin(k).wait_send()
        for j in range(len(SCATTER)):
            scatter(j).wait_send()

    for copy in sent[:-1]:
        copy.wait_send()
    del sent[:-1]
    for q in range(4):
        for dy in (1, 0):
            @pl.when((dy == 1) | (q != z % 4))
            def _():
                to_owner(q, dy).wait_send()
    for k in (1, 3):
        send(far.at[zh], far.at[zh], d3s.at[k], d3r.at[zh], dev((z + 4 * k) % NZ, yl, core, m))
    for k in (1, 3, 2):
        arrived(far.at[(zh + k) % 4], d3r.at[(zh + k) % 4])
    total = far[0].astype(F32)
    for i in range(1, 4):
        total += far[i].astype(F32)
    own = 2 * (z % 4) + yl
    cres[core, own] = (total * factor).astype(BF16)
    place = cres.at[core, own]
    for i in (3, 1, 2, 0):
        zu = (z - sign * NEAR[i] + NZ) % NZ
        for dy in (1, 0):
            if i > 0 or dy == 1:
                send(place, place, d4s.at[i, dy], d4r.at[i, yl], dev(zu, (yl + dy) % 2, core, m))
    send(place, place, d5s.at[0, 0], d5r.at[0, 0], sibling)
    for i in (0, 1, 2, 3):
        zo = (z + sign * NEAR[i] + NZ) % NZ
        for dy in (0, 1):
            if i > 0 or dy == 1:
                yo = (yl + dy) % 2
                place = cres.at[core, 2 * (zo % 4) + yo]
                arrived(place, d4r.at[i, yo])
                send(place, place, d5s.at[i, dy], d5r.at[i, dy], sibling)
    for i in (0, 1, 2, 3):
        zo = (z - sign * NEAR[i] + NZ) % NZ
        for dy in (0, 1):
            arrived(cres.at[1 - core, 2 * (zo % 4) + (yl + dy) % 2], d5r.at[i, dy])

    for copy in sent:
        copy.wait_send()


def step(m_ref, c_ref, p_ref, w_ref, m_out, w_out, mom, wei, sem):
    copies = []

    def leave(src, dst, i):
        copies.append(pltpu.make_async_copy(src, dst, sem.at[i]))
        copies[-1].start()

    tiles = [slice(128 * k, 128 * (k + 1)) for k in range(COLS // 128)]
    for k, rows in enumerate(tiles):
        mom[rows] = 0.9 * m_ref[rows] + c_ref[:, rows].T.astype(F32)
        leave(mom.at[rows], m_out.at[rows], k)
    for k, rows in enumerate(tiles):
        update = lax.dot_general(
            p_ref[...], mom[rows].astype(BF16), (((1,), (1,)), ((), ())), preferred_element_type=F32
        )
        wei[:, rows] = (w_ref[:, rows].astype(F32) - 2.0 * update).astype(BF16)
        leave(wei.at[:, rows], w_out.at[:, rows], len(tiles) + k)
    for copy in copies:
        copy.wait()


def shards(attn_out, out_grad, projection, momentum, weight):
    factor = 1.0 / math.sqrt(attn_out.shape[0] * lax.axis_size("dp"))
    vmem, dma = pltpu.VMEM, pltpu.SemaphoreType.DMA
    compressed = pl.pallas_call(
        functools.partial(kernel, factor),
        out_shape=jax.ShapeDtypeStruct((2, CHUNKS, SL, COLS), BF16),
        in_specs=[pl.BlockSpec(memory_space=pltpu.HBM)] * 3,
        out_specs=pl.BlockSpec(memory_space=vmem),
        scratch_shapes=[
            vmem((2, TOK, COLS), BF16), vmem((TOK, COLS), BF16), vmem((BLK, RANK), BF16),
            vmem((2, SLICES, 2, 2, SL, TOK), BF16), vmem((2, NM, 2, 2, SL, TOK), BF16), vmem((2, NZ, SL, RANK), BF16),
            vmem((2, RANK, TOK), F32), vmem((2, RANK, TOK), BF16), vmem((2, SLICES, PIECE, TOK), BF16),
            vmem((PIECE, TOK), BF16), vmem((2, HALF, TOK), BF16),
            vmem((CHUNKS, SL, COLS), BF16), vmem((4, 2, SL, COLS), BF16), vmem((4, SL, COLS), BF16),
            dma((3,)),
            dma((NZ,)), dma((3, 5)), dma((NZ,)), dma((15,)), dma((2, NM)), dma((NZ,)), dma((NZ,)), dma, dma,
            dma((15,)), dma((2, SLICES)), dma((NM,)), dma((2, 4)),
            dma((4, 2)), dma((4, 2)), dma((4,)), dma((4,)),
            dma((4, 2)), dma((4, 2)), dma((4, 2)), dma((4, 2)),
        ],
        compiler_params=pltpu.CompilerParams(
            collective_id=0, has_side_effects=True, vmem_limit_bytes=213 * 2**18
        ),
        cost_estimate=pl.CostEstimate(flops=300_000_000, bytes_accessed=4_000_000, transcendentals=0),
        name="compress",
    )(attn_out, out_grad, projection)
    new_momentum, new_weight = pl.pallas_call(
        step,
        out_shape=(
            jax.ShapeDtypeStruct((COLS, RANK), F32),
            jax.ShapeDtypeStruct((BLK, COLS), BF16),
        ),
        in_specs=[pl.BlockSpec(memory_space=vmem)] * 4,
        out_specs=(pl.BlockSpec(memory_space=pltpu.HBM), pl.BlockSpec(memory_space=pltpu.HBM)),
        scratch_shapes=[vmem((COLS, RANK), F32), vmem((BLK, COLS), BF16), dma((2 * COLS // 128,))],
        compiler_params=pltpu.CompilerParams(vmem_limit_bytes=16 * 2**20),
        cost_estimate=pl.CostEstimate(flops=51_000_000, bytes_accessed=3_000_000, transcendentals=0),
        name="momentum_and_weight",
    )(momentum, compressed.reshape(RANK, COLS), projection, weight.T)
    return (new_momentum, new_weight.T)


def solution(mesh):
    return jax.shard_map(
        shards,
        mesh=mesh,
        in_specs=(P("dp", "mp"), P("dp", "mp"), P("dp", None), P("mp", None), P("mp", "dp")),
        out_specs=(P("mp", None), P("mp", "dp")),
        check_vma=False,
    )
```

time: 62.9 us -> 60.6 us (0.963)
  Pallas kernels: 61.2 us -> 58.9 us
    pallas_call x1, Pallas kernels: 59.4 us -> 57.7 us  [shards(): pl.pallas_call(functools.partial(kernel, factor), out_shape=jax.ShapeDtyp...]
    pallas_call x1, Pallas kernels: 1.84 us -> 1.16 us  [shards(): pl.pallas_call(step, out_shape=(jax.ShapeDtypeStruct((COLS, RANK), F32),...]
where the time goes in v5:
time: 60.6 us; the launch traced here: 60.4 us
  Pallas kernels  58.9 us (97%)
  local copies, waits for them, and re-layouts  0.9 us (1%)
  between operations  0.67 us (1%)
    pallas_call x1, Pallas kernels, shards(): pl.pallas_call(functools.partial(kernel, factor), out_shape=jax.ShapeDtyp...  57.7 us

profile of v5, /device:TPU:1, one launch (start us, length us, event | category | flops | bytes accessed | tf_op | source)
XLA Modules:
  0.0 60.4 jit_solution(678062209613738394)
XLA Ops:
  0.6 0.0 copy-start
  0.6 0.0 copy-start.1
  0.7 0.9 %copy-done.1 = bf16[112,256]{1,0:T(8,128)(2,1)S(1)} copy-done((bf16[112,256]{1,0:T(8,128)(2,1)S(1)}, bf16[112,256]{1,0:T(8,128)(2,1)}, u32[]{:S(2)}) %copy-start.1) | copy-done | bytes 57368
  1.5 0.0 copy-start.2
  1.5 57.7 %compress.1 = bf16[2,8,16,896]{3,2,1,0:T(8,128)(2,1)S(1)} custom-call(bf16[256,896]{1,0:T(8,128)(2,1)} %a_hbm.1, bf16[256,896]{1,0:T(8,128)(2,1)} %g_hbm.1, bf16[112,256]{1,0:T(8,128)(2,1)S(1)} %copy-done.1), custom_call_target="tpu_custom_call" | custom-call | flops 300000000 | bytes 4000000 | tf_op jit(solution)/shard_map/compress/pallas_call | solution.py:330
  59.2 0.0 copy-done
  59.3 0.0 copy-done.2
  59.3 1.2 %momentum_and_weight.1 = (f32[896,256]{1,0:T(8,128)}, bf16[112,896]{1,0:T(8,128)(2,1)}) custom-call(f32[896,256]{1,0:T(8,128)S(1)} %copy-done, bf16[256,896]{1,0:T(8,128)(2,1)S(1)} %bitcast.3, bf16[112,256]{1,0:T(8,128)(2,1)S(1)} %copy-done.1, bf16[112,896]{1,0:T(8,128)(2,1)S(1)} %bitcast.4), custom_call_target="tpu_custom_call" | custom-call | flops 51000000 | bytes 3000000 | tf_op jit(solution)/shard_map/momentum_and_weight/pallas_call | solution.py:353
Async XLA Ops:
  0.6 58.6 %copy-start = (f32[896,256]{1,0:T(8,128)S(1)}, f32[896,256]{1,0:T(8,128)}, u32[]{:S(2)}) copy-start(f32[896,256]{1,0:T(8,128)} %m_ref.1) | copy-start | bytes 2752516
  0.6 0.9 %copy-start.1 = (bf16[112,256]{1,0:T(8,128)(2,1)S(1)}, bf16[112,256]{1,0:T(8,128)(2,1)}, u32[]{:S(2)}) copy-start(bf16[112,256]{1,0:T(8,128)(2,1)} %p_ref.1) | copy-start | bytes 172036
  1.5 57.7 %copy-start.2 = (bf16[896,112]{0,1:T(8,128)(2,1)S(1)}, bf16[896,112]{0,1:T(8,128)(2,1)}, u32[]{:S(2)}) copy-start(bf16[896,112]{0,1:T(8,128)(2,1)} %param.9) | copy-start | bytes 602116

commit v6 on v5

--- a/solution.py
+++ b/solution.py
@@ -345,11 +345,11 @@
             dma((4, 2)), dma((4, 2)), dma((4, 2)), dma((4, 2)),
         ],
         compiler_params=pltpu.CompilerParams(
-            collective_id=0, has_side_effects=True, vmem_limit_bytes=213 * 2**18
+            collective_id=0, has_side_effects=True, vmem_limit_bytes=32 * 2**20
         ),
         cost_estimate=pl.CostEstimate(flops=300_000_000, bytes_accessed=4_000_000, transcendentals=0),
         name="compress",
-    )(attn_out, out_grad, projection)
+    )(*(pltpu.with_memory_space_constraint(x, pltpu.HBM) for x in (attn_out, out_grad, projection)))
     new_momentum, new_weight = pl.pallas_call(
         step,
         out_shape=(

time: 60.6 us -> 59.6 us (0.983)
  local copies, waits for them, and re-layouts: 0.9 us -> 0.01 us
    unnamed x6, local copies, waits for them, and re-layouts: 0.9 us -> 0.01 us
where the time goes in v6:
time: 59.6 us; the launch traced here: 59.5 us
  Pallas kernels  58.8 us (99%)
  between operations  0.69 us (1%)
    pallas_call x1, Pallas kernels, shards(): pl.pallas_call(functools.partial(kernel, factor), out_shape=jax.ShapeDtyp...  57.6 us

profile of v6, /device:TPU:1, one launch (start us, length us, event | category | flops | bytes accessed | tf_op | source)
XLA Modules:
  0.0 59.5 jit_solution(12039681366700500974)
XLA Ops:
  0.6 0.0 copy-start
  0.6 0.0 copy-start.1
  0.7 0.0 copy-start.2
  0.7 57.6 %compress.1 = bf16[2,8,16,896]{3,2,1,0:T(8,128)(2,1)S(1)} custom-call(bf16[256,896]{1,0:T(8,128)(2,1)} %a_hbm.1, bf16[256,896]{1,0:T(8,128)(2,1)} %g_hbm.1, bf16[112,256]{1,0:T(8,128)(2,1)} %p_ref.1), custom_call_target="tpu_custom_call" | custom-call | flops 300000000 | bytes 4000000 | tf_op jit(solution)/shard_map/compress/pallas_call | solution.py:330
  58.3 0.0 copy-done
  58.3 0.0 copy-done.1
  58.3 0.0 copy-done.2
  58.3 1.2 %momentum_and_weight.1 = (f32[896,256]{1,0:T(8,128)}, bf16[112,896]{1,0:T(8,128)(2,1)}) custom-call(f32[896,256]{1,0:T(8,128)S(1)} %copy-done, bf16[256,896]{1,0:T(8,128)(2,1)S(1)} %bitcast.3, bf16[112,256]{1,0:T(8,128)(2,1)S(1)} %copy-done.1, bf16[112,896]{1,0:T(8,128)(2,1)S(1)} %bitcast.4), custom_call_target="tpu_custom_call" | custom-call | flops 51000000 | bytes 3000000 | tf_op jit(solution)/shard_map/momentum_and_weight/pallas_call | solution.py:353
Async XLA Ops:
  0.6 57.7 %copy-start = (f32[896,256]{1,0:T(8,128)S(1)}, f32[896,256]{1,0:T(8,128)}, u32[]{:S(2)}) copy-start(f32[896,256]{1,0:T(8,128)} %m_ref.1) | copy-start | bytes 2752516
  0.6 57.7 %copy-start.1 = (bf16[112,256]{1,0:T(8,128)(2,1)S(1)}, bf16[112,256]{1,0:T(8,128)(2,1)}, u32[]{:S(2)}) copy-start(bf16[112,256]{1,0:T(8,128)(2,1)} %p_ref.1) | copy-start | bytes 172036
  0.7 57.7 %copy-start.2 = (bf16[896,112]{0,1:T(8,128)(2,1)S(1)}, bf16[896,112]{0,1:T(8,128)(2,1)}, u32[]{:S(2)}) copy-start(bf16[896,112]{0,1:T(8,128)(2,1)} %param.9) | copy-start | bytes 602116

commit v7 on v6

--- a/solution.py
+++ b/solution.py
@@ -19,6 +19,7 @@
 TOK, COLS, RANK = 256, 896, 256
 HALF = RANK // 2
 PIECE = TOK // NM
+PARTS = (slice(0, 512), slice(512, COLS))
 CHUNKS = HALF // SL
 NEAR = (0, 1, -1, -2)
 REACH = (4, 12, 3, 13, 2, 14, 1, 15)
@@ -113,7 +114,7 @@
 
     @pl.when(m < SLICES)
     def _():
-        for k in REACH[:2]:
+        for k in REACH:
             along(k).start()
         pz[core, z] = p[cut]
         twin(z).start()
@@ -140,8 +141,6 @@
             for k in steps:
                 onward(way, k).start()
             twin(source).start()
-        for k in REACH[2:]:
-            along(k).start()
 
 
     def piece(i):
@@ -239,7 +238,10 @@
     for i in (1, 2, 3):
         total += rs2[i, 0].astype(F32) + rs2[i, 1].astype(F32)
     far[zh] = total.astype(BF16)
-    send(far.at[zh], far.at[zh], d3s.at[2], d3r.at[zh], dev((z + 8) % NZ, yl, core, m))
+    for b, lanes in enumerate(PARTS):
+        for k in (2, 1, 3):
+            place = far.at[zh, :, lanes]
+            send(place, place, d3s.at[b, k], d3r.at[b, zh], dev((z + 4 * k) % NZ, yl, core, m))
 
     for j, (mt, _) in enumerate(plane):
         @pl.when(mt < SLICES)
@@ -262,42 +264,43 @@
         for j in range(len(SCATTER)):
             scatter(j).wait_send()
 
-    for copy in sent[:-1]:
+    for copy in sent[:-6]:
         copy.wait_send()
-    del sent[:-1]
+    del sent[:-6]
     for q in range(4):
         for dy in (1, 0):
             @pl.when((dy == 1) | (q != z % 4))
             def _():
                 to_owner(q, dy).wait_send()
-    for k in (1, 3):
-        send(far.at[zh], far.at[zh], d3s.at[k], d3r.at[zh], dev((z + 4 * k) % NZ, yl, core, m))
-    for k in (1, 3, 2):
-        arrived(far.at[(zh + k) % 4], d3r.at[(zh + k) % 4])
-    total = far[0].astype(F32)
-    for i in range(1, 4):
-        total += far[i].astype(F32)
     own = 2 * (z % 4) + yl
-    cres[core, own] = (total * factor).astype(BF16)
-    place = cres.at[core, own]
-    for i in (3, 1, 2, 0):
-        zu = (z - sign * NEAR[i] + NZ) % NZ
-        for dy in (1, 0):
-            if i > 0 or dy == 1:
-                send(place, place, d4s.at[i, dy], d4r.at[i, yl], dev(zu, (yl + dy) % 2, core, m))
-    send(place, place, d5s.at[0, 0], d5r.at[0, 0], sibling)
-    for i in (0, 1, 2, 3):
-        zo = (z + sign * NEAR[i] + NZ) % NZ
-        for dy in (0, 1):
-            if i > 0 or dy == 1:
-                yo = (yl + dy) % 2
-                place = cres.at[core, 2 * (zo % 4) + yo]
-                arrived(place, d4r.at[i, yo])
-                send(place, place, d5s.at[i, dy], d5r.at[i, dy], sibling)
-    for i in (0, 1, 2, 3):
-        zo = (z - sign * NEAR[i] + NZ) % NZ
-        for dy in (0, 1):
-            arrived(cres.at[1 - core, 2 * (zo % 4) + (yl + dy) % 2], d5r.at[i, dy])
+    for b, lanes in enumerate(PARTS):
+        for k in (1, 3, 2):
+            arrived(far.at[(zh + k) % 4, :, lanes], d3r.at[b, (zh + k) % 4])
+        total = far[0, :, lanes].astype(F32)
+        for i in range(1, 4):
+            total += far[i, :, lanes].astype(F32)
+        cres[core, own, :, lanes] = (total * factor).astype(BF16)
+        place = cres.at[core, own, :, lanes]
+        for i in (3, 1, 2, 0):
+            zu = (z - sign * NEAR[i] + NZ) % NZ
+            for dy in (1, 0):
+                if i > 0 or dy == 1:
+                    send(place, place, d4s.at[b, i, dy], d4r.at[b, i, yl], dev(zu, (yl + dy) % 2, core, m))
+        send(place, place, d5s.at[b, 0, 0], d5r.at[b, 0, 0], sibling)
+    for b, lanes in enumerate(PARTS):
+        for i in (0, 1, 2, 3):
+            zo = (z + sign * NEAR[i] + NZ) % NZ
+            for dy in (0, 1):
+                if i > 0 or dy == 1:
+                    yo = (yl + dy) % 2
+                    place = cres.at[core, 2 * (zo % 4) + yo, :, lanes]
+                    arrived(place, d4r.at[b, i, yo])
+                    send(place, place, d5s.at[b, i, dy], d5r.at[b, i, dy], sibling)
+    for b, lanes in enumerate(PARTS):
+        for i in (0, 1, 2, 3):
+            zo = (z - sign * NEAR[i] + NZ) % NZ
+            for dy in (0, 1):
+                arrived(cres.at[1 - core, 2 * (zo % 4) + (yl + dy) % 2, :, lanes], d5r.at[b, i, dy])
 
     for copy in sent:
         copy.wait_send()
@@ -341,8 +344,8 @@
             dma((3,)),
             dma((NZ,)), dma((3, 5)), dma((NZ,)), dma((15,)), dma((2, NM)), dma((NZ,)), dma((NZ,)), dma, dma,
             dma((15,)), dma((2, SLICES)), dma((NM,)), dma((2, 4)),
-            dma((4, 2)), dma((4, 2)), dma((4,)), dma((4,)),
-            dma((4, 2)), dma((4, 2)), dma((4, 2)), dma((4, 2)),
+            dma((4, 2)), dma((4, 2)), dma((2, 4)), dma((2, 4)),
+            dma((2, 4, 2)), dma((2, 4, 2)), dma((2, 4, 2)), dma((2, 4, 2)),
         ],
         compiler_params=pltpu.CompilerParams(
             collective_id=0, has_side_effects=True, vmem_limit_bytes=32 * 2**20

time: 59.6 us -> 59.3 us (level)
  no operation moved by 1% of the time
where the time goes in v7:
time: 59.3 us; the launch traced here: 59.2 us
  Pallas kernels  58.5 us (99%)
  between operations  0.69 us (1%)
    pallas_call x1, Pallas kernels, shards(): pl.pallas_call(functools.partial(kernel, factor), out_shape=jax.ShapeDtyp...  57.3 us

profile of v7, /device:TPU:1, one launch (start us, length us, event | category | flops | bytes accessed | tf_op | source)
XLA Modules:
  0.0 59.2 jit_solution(18387037363161879590)
XLA Ops:
  0.6 0.0 copy-start
  0.6 0.0 copy-start.1
  0.7 0.0 copy-start.2
  0.7 57.3 %compress.1 = bf16[2,8,16,896]{3,2,1,0:T(8,128)(2,1)S(1)} custom-call(bf16[256,896]{1,0:T(8,128)(2,1)} %a_hbm.1, bf16[256,896]{1,0:T(8,128)(2,1)} %g_hbm.1, bf16[112,256]{1,0:T(8,128)(2,1)} %p_ref.1), custom_call_target="tpu_custom_call" | custom-call | flops 300000000 | bytes 4000000 | tf_op jit(solution)/shard_map/compress/pallas_call | solution.py:333
  58.0 0.0 copy-done
  58.0 0.0 copy-done.1
  58.0 0.0 copy-done.2
  58.0 1.2 %momentum_and_weight.1 = (f32[896,256]{1,0:T(8,128)}, bf16[112,896]{1,0:T(8,128)(2,1)}) custom-call(f32[896,256]{1,0:T(8,128)S(1)} %copy-done, bf16[256,896]{1,0:T(8,128)(2,1)S(1)} %bitcast.3, bf16[112,256]{1,0:T(8,128)(2,1)S(1)} %copy-done.1, bf16[112,896]{1,0:T(8,128)(2,1)S(1)} %bitcast.4), custom_call_target="tpu_custom_call" | custom-call | flops 51000000 | bytes 3000000 | tf_op jit(solution)/shard_map/momentum_and_weight/pallas_call | solution.py:356
Async XLA Ops:
  0.6 57.4 %copy-start = (f32[896,256]{1,0:T(8,128)S(1)}, f32[896,256]{1,0:T(8,128)}, u32[]{:S(2)}) copy-start(f32[896,256]{1,0:T(8,128)} %m_ref.1) | copy-start | bytes 2752516
  0.6 57.4 %copy-start.1 = (bf16[112,256]{1,0:T(8,128)(2,1)S(1)}, bf16[112,256]{1,0:T(8,128)(2,1)}, u32[]{:S(2)}) copy-start(bf16[112,256]{1,0:T(8,128)(2,1)} %p_ref.1) | copy-start | bytes 172036
  0.7 57.4 %copy-start.2 = (bf16[896,112]{0,1:T(8,128)(2,1)S(1)}, bf16[896,112]{0,1:T(8,128)(2,1)}, u32[]{:S(2)}) copy-start(bf16[896,112]{0,1:T(8,128)(2,1)} %param.9) | copy-start | bytes 602116

commit v8 on v7

--- a/solution.py
+++ b/solution.py
@@ -19,7 +19,7 @@
 TOK, COLS, RANK = 256, 896, 256
 HALF = RANK // 2
 PIECE = TOK // NM
-PARTS = (slice(0, 512), slice(512, COLS))
+PARTS = (slice(0, 384), slice(384, 640), slice(640, COLS))
 CHUNKS = HALF // SL
 NEAR = (0, 1, -1, -2)
 REACH = (4, 12, 3, 13, 2, 14, 1, 15)
@@ -264,9 +264,9 @@
         for j in range(len(SCATTER)):
             scatter(j).wait_send()
 
-    for copy in sent[:-6]:
+    for copy in sent[:-9]:
         copy.wait_send()
-    del sent[:-6]
+    del sent[:-9]
     for q in range(4):
         for dy in (1, 0):
             @pl.when((dy == 1) | (q != z % 4))
@@ -344,8 +344,8 @@
             dma((3,)),
             dma((NZ,)), dma((3, 5)), dma((NZ,)), dma((15,)), dma((2, NM)), dma((NZ,)), dma((NZ,)), dma, dma,
             dma((15,)), dma((2, SLICES)), dma((NM,)), dma((2, 4)),
-            dma((4, 2)), dma((4, 2)), dma((2, 4)), dma((2, 4)),
-            dma((2, 4, 2)), dma((2, 4, 2)), dma((2, 4, 2)), dma((2, 4, 2)),
+            dma((4, 2)), dma((4, 2)), dma((3, 4)), dma((3, 4)),
+            dma((3, 4, 2)), dma((3, 4, 2)), dma((3, 4, 2)), dma((3, 4, 2)),
         ],
         compiler_params=pltpu.CompilerParams(
             collective_id=0, has_side_effects=True, vmem_limit_bytes=32 * 2**20

time: 59.3 us -> 59.8 us (level)
  no operation moved by 1% of the time
where the time goes in v8:
time: 59.8 us; the launch traced here: 59.6 us
  Pallas kernels  58.9 us (98%)
  between operations  0.69 us (1%)
    pallas_call x1, Pallas kernels, shards(): pl.pallas_call(functools.partial(kernel, factor), out_shape=jax.ShapeDtyp...  57.8 us

profile of v8, /device:TPU:1, one launch (start us, length us, event | category | flops | bytes accessed | tf_op | source)
XLA Modules:
  0.0 59.6 jit_solution(11673498127863443341)
XLA Ops:
  0.6 0.0 copy-start
  0.6 0.0 copy-start.1
  0.7 0.0 copy-start.2
  0.7 57.8 %compress.1 = bf16[2,8,16,896]{3,2,1,0:T(8,128)(2,1)S(1)} custom-call(bf16[256,896]{1,0:T(8,128)(2,1)} %a_hbm.1, bf16[256,896]{1,0:T(8,128)(2,1)} %g_hbm.1, bf16[112,256]{1,0:T(8,128)(2,1)} %p_ref.1), custom_call_target="tpu_custom_call" | custom-call | flops 300000000 | bytes 4000000 | tf_op jit(solution)/shard_map/compress/pallas_call | solution.py:333
  58.5 0.0 copy-done
  58.5 0.0 copy-done.1
  58.5 0.0 copy-done.2
  58.5 1.2 %momentum_and_weight.1 = (f32[896,256]{1,0:T(8,128)}, bf16[112,896]{1,0:T(8,128)(2,1)}) custom-call(f32[896,256]{1,0:T(8,128)S(1)} %copy-done, bf16[256,896]{1,0:T(8,128)(2,1)S(1)} %bitcast.3, bf16[112,256]{1,0:T(8,128)(2,1)S(1)} %copy-done.1, bf16[112,896]{1,0:T(8,128)(2,1)S(1)} %bitcast.4), custom_call_target="tpu_custom_call" | custom-call | flops 51000000 | bytes 3000000 | tf_op jit(solution)/shard_map/momentum_and_weight/pallas_call | solution.py:356
Async XLA Ops:
  0.6 57.8 %copy-start = (f32[896,256]{1,0:T(8,128)S(1)}, f32[896,256]{1,0:T(8,128)}, u32[]{:S(2)}) copy-start(f32[896,256]{1,0:T(8,128)} %m_ref.1) | copy-start | bytes 2752516
  0.6 57.8 %copy-start.1 = (bf16[112,256]{1,0:T(8,128)(2,1)S(1)}, bf16[112,256]{1,0:T(8,128)(2,1)}, u32[]{:S(2)}) copy-start(bf16[112,256]{1,0:T(8,128)(2,1)} %p_ref.1) | copy-start | bytes 172036
  0.7 57.8 %copy-start.2 = (bf16[896,112]{0,1:T(8,128)(2,1)S(1)}, bf16[896,112]{0,1:T(8,128)(2,1)}, u32[]{:S(2)}) copy-start(bf16[896,112]{0,1:T(8,128)(2,1)} %param.9) | copy-start | bytes 602116
